TPU v7x, 128 devices: a whole 4x4x4 slice. The times are simulated.
128 devices in a mesh: dp: 4 (over z_hi, core), expert: 32 (over y, x, z_lo).
Axes of the slice: x: 4, y: 4, z: 4 (z_hi: 2, z_lo: 2; z = z_hi * 2 + z_lo), core: 2. Of those that a mesh axis runs over, the one named last changes fastest.
Arguments:
- tokens: bfloat16 [256, 512, 1408], P(('dp', 'expert')), may hold values from -6 to 6
- slot_keys: bfloat16 [1408, 32], replicated, may hold values from -6 to 6
- logit_scale: float32 [1], replicated, may hold values from 20 to 40
- w_in: bfloat16 [32, 1408, 6144], P('expert', None, 'dp'), may hold values from -6 to 6
- w_out: bfloat16 [32, 6144, 1408], P('expert', 'dp'), may hold values from -0.078125 to 0.078125
- grad_out: bfloat16 [256, 512, 1408], P(('dp', 'expert')), may hold values from -6 to 6
Outputs:
- grad_tokens: bfloat16 [256, 512, 1408], P(('dp', 'expert'))
- grad_in: bfloat16 [32, 1408, 6144], P('expert', None, 'dp')
- grad_outw: bfloat16 [32, 6144, 1408], P('expert', 'dp')
- grad_keys: float32 [1408, 32], P(None, 'expert')
All inputs are finite; a program needn't handle non-finite values.
Results may differ from a plain program's by a relative error of at most 0.011.
Values may be sent and summed in bfloat16 or wider, within the bound.
A program may use at most 128 MiB of HBM per device.

v0:
```python
import jax
import jax.numpy as jnp
from jax import lax
from jax.sharding import PartitionSpec as P

EPS = 1e-06


def normalize(v, axis):
    return v * lax.rsqrt(jnp.sum(v * v, axis=axis, keepdims=True) + EPS)


def gelu_exact(v):
    return 0.5 * v * (1.0 + lax.erf(v * 0.7071067811865476))


def gelu_slope(v):
    return (
        0.5 * (1.0 + lax.erf(v * 0.7071067811865476))
        + v * jnp.exp(-0.5 * v * v) * 0.3989422804014327
    )


def body(tokens, slot_keys, logit_scale, w_in, w_out, grad_out):
    scale = logit_scale[0]
    width = tokens.shape[2]
    key_float = slot_keys.astype(jnp.float32)
    keys = normalize(key_float, 0).astype(jnp.bfloat16)
    token_float = tokens.astype(jnp.float32)
    normed = normalize(token_float, -1).astype(jnp.bfloat16)
    expo = jnp.exp(
        scale * jnp.einsum("btd,ds->bts", normed, keys, preferred_element_type=jnp.float32)
    )
    dispatch = expo / jnp.sum(expo, axis=1, keepdims=True)
    combine = expo / jnp.sum(expo, axis=2, keepdims=True)
    dispatch_b = dispatch.astype(jnp.bfloat16)
    combine_b = combine.astype(jnp.bfloat16)
    slot_in = jnp.einsum(
        "bts,btd->bsd", dispatch_b, tokens, preferred_element_type=jnp.float32
    ).astype(jnp.bfloat16)
    slot_grad = jnp.einsum(
        "bts,btd->bsd", combine_b, grad_out, preferred_element_type=jnp.float32
    ).astype(jnp.bfloat16)
    sent_in, sent_grad = (
        lax.all_to_all(slot_in, "expert", split_axis=1, concat_axis=0, tiled=True),
        lax.all_to_all(slot_grad, "expert", split_axis=1, concat_axis=0, tiled=True),
    )
    whole_in, whole_grad = (
        lax.all_gather(sent_in, "dp", axis=0, tiled=True),
        lax.all_gather(sent_grad, "dp", axis=0, tiled=True),
    )
    inputs = whole_in[:, 0, :]
    grads = whole_grad[:, 0, :]
    first = w_in[0]
    second = w_out[0]
    pre = jnp.dot(inputs, first, preferred_element_type=jnp.float32)
    act = gelu_exact(pre).astype(jnp.bfloat16)
    hidden_grad = lax.dot_general(
        grads, second, (((1,), (1,)), ((), ())), preferred_element_type=jnp.float32
    )
    pre_grad = (hidden_grad * gelu_slope(pre)).astype(jnp.bfloat16)
    second_grad = lax.dot_general(
        act, grads, (((0,), (0,)), ((), ())), preferred_element_type=jnp.float32
    )
    first_grad = lax.dot_general(
        inputs, pre_grad, (((0,), (0,)), ((), ())), preferred_element_type=jnp.float32
    )
    out_term = jnp.dot(act, second, preferred_element_type=jnp.float32)
    back_term = lax.dot_general(
        pre_grad, first, (((1,), (1,)), ((), ())), preferred_element_type=jnp.float32
    )
    summed = lax.psum_scatter(
        jnp.concatenate([out_term, back_term], axis=1), "dp", scatter_dimension=0, tiled=True
    )
    out_rows = summed[:, :width].astype(jnp.bfloat16)[:, None, :]
    back_rows = summed[:, width:].astype(jnp.bfloat16)[:, None, :]
    slot_out, slot_back = (
        lax.all_to_all(out_rows, "expert", split_axis=0, concat_axis=1, tiled=True),
        lax.all_to_all(back_rows, "expert", split_axis=0, concat_axis=1, tiled=True),
    )
    comb_grad = jnp.einsum("btd,bsd->bts", grad_out, slot_out, preferred_element_type=jnp.float32)
    disp_grad = jnp.einsum("btd,bsd->bts", tokens, slot_back, preferred_element_type=jnp.float32)
    direct = jnp.einsum("bts,bsd->btd", dispatch_b, slot_back, preferred_element_type=jnp.float32)
    logit_grad = dispatch * (disp_grad - jnp.sum(dispatch * disp_grad, axis=1, keepdims=True))
    logit_grad = logit_grad + combine * (
        comb_grad - jnp.sum(combine * comb_grad, axis=2, keepdims=True)
    )
    logit_grad = logit_grad.astype(jnp.bfloat16)
    normed_grad = scale * jnp.einsum(
        "bts,ds->btd", logit_grad, keys, preferred_element_type=jnp.float32
    )
    keys_local = scale * jnp.einsum(
        "btd,bts->ds", normed, logit_grad, preferred_element_type=jnp.float32
    )
    _, pullback = jax.vjp(lambda v: normalize(v, -1), token_float)
    grad_tokens = (direct + pullback(normed_grad)[0]).astype(jnp.bfloat16)
    columns = keys_local.shape[1] // lax.axis_size("expert")
    keys_total = lax.psum(keys_local, ("dp", "expert"))
    keys_mine = lax.dynamic_slice_in_dim(keys_total, lax.axis_index("expert") * columns, columns, 1)
    own_keys = lax.dynamic_slice_in_dim(key_float, lax.axis_index("expert") * columns, columns, 1)
    _, key_pullback = jax.vjp(lambda v: normalize(v, 0), own_keys)
    grad_keys = key_pullback(keys_mine)[0]
    return (
        grad_tokens,
        first_grad.astype(jnp.bfloat16)[None],
        second_grad.astype(jnp.bfloat16)[None],
        grad_keys,
    )


def solution(mesh):
    in_specs = (
        P(("dp", "expert"), None, None),
        P(),
        P(),
        P("expert", None, "dp"),
        P("expert", "dp", None),
        P(("dp", "expert"), None, None),
    )
    out_specs = (
        P(("dp", "expert"), None, None),
        P("expert", None, "dp"),
        P("expert", "dp", None),
        P(None, "expert"),
    )
    return jax.shard_map(body, mesh=mesh, in_specs=in_specs, out_specs=out_specs, check_vma=False)
```

profile of v0, /device:TPU:1, one launch (start us, length us, event | category | flops | bytes accessed | tf_op | source)
XLA Modules:
  0.0 310.7 jit_solution(14410919963100647266)
XLA Ops:
  7.2 2.6 fusion.6
  12.0 1.1 fusion.40
  14.8 9.2 %all-to-all-start = ((bf16[2,32,1408]{2,0,1:T(2,128)(2,1)}), bf16[2,32,1408]{2,0,1:T(2,128)(2,1)S(1)}, u32[]{:S(2)}, u32[]{:S(2)}) async-start(bf16[2,32,1408]{2,0,1:T(2,128)(2,1)} %copy.20), calls=%async_computation | async-start | bytes 360448 | tf_op jit(solution)/shard_map/all_to_all | solution.py:45
  24.0 1.6 convolution_convert_fusion.2
  26.4 5.5 %all-to-all-done = bf16[2,32,1408]{2,0,1:T(2,128)(2,1)S(1)} async-done(((bf16[2,32,1408]{2,0,1:T(2,128)(2,1)}), bf16[2,32,1408]{2,0,1:T(2,128)(2,1)S(1)}, u32[]{:S(2)}, u32[]{:S(2)}) %all-to-all-start) | async-done | bytes 180256 | tf_op jit(solution)/shard_map/all_to_all | solution.py:45
  31.9 4.6 %all-to-all-start.1 = ((bf16[2,32,1408]{2,0,1:T(2,128)(2,1)}), bf16[2,32,1408]{2,0,1:T(2,128)(2,1)}, u32[]{:S(2)}, u32[]{:S(2)}) async-start(bf16[2,32,1408]{2,0,1:T(2,128)(2,1)} %copy.21), calls=%async_computation.1 | async-start | bytes 360448 | tf_op jit(solution)/shard_map/all_to_all | solution.py:46
  36.6 14.0 %all_gather.6 = bf16[256,1,1408]{2,0,1:T(8,128)(2,1)} all-gather(bf16[64,1,1408]{2,0,1:T(8,128)(2,1)S(1)} %all_to_all.55), channel_id=1, replica_groups=mesh['dp'=4,'expert'=32] {'dp'}, dimensions={0}, use_global_device_ids=true | all-gather | bytes 901120 | tf_op jit(solution)/shard_map/all_gather | solution.py:49
  51.6 9.9 %all_gather.7 = bf16[256,1,1408]{2,0,1:T(8,128)(2,1)S(1)} all-gather(bf16[64,1,1408]{2,0,1:T(8,128)(2,1)S(1)} %all_to_all.59), channel_id=1, replica_groups=mesh['dp'=4,'expert'=32] {'dp'}, dimensions={0}, use_global_device_ids=true | all-gather | bytes 901120 | tf_op jit(solution)/shard_map/all_gather | solution.py:50
  61.5 4.1 %fusion.15 = f32[256,1536]{1,0:T(8,128)S(1)} fusion(bf16[1,1408,1536]{2,1,0:T(8,128)(2,1)} %param.9, bf16[256,1,1408]{2,0,1:T(8,128)(2,1)} %all_gather.6), kind=kOutput, calls=%fused_computation.22 | convolution fusion | flops 1107296256 | bytes 6619136 | tf_op jit(solution)/shard_map/dot_general | solution.py:56
  65.7 4.2 %fusion.11 = f32[256,1408]{1,0:T(8,128)S(1)} fusion(bf16[1,1536,1408]{2,1,0:T(8,128)(2,1)} %param.10, f32[256,1536]{1,0:T(8,128)S(1)} %fusion.15), kind=kOutput, calls=%fused_computation.18 | convolution fusion | flops 1109262336 | bytes 7340032 | tf_op jit(solution)/shard_map/dot_general | solution.py:68
  69.9 1.6 fusion.20
  71.5 1.4 fusion.13
  73.0 1.8 pad_maximum_fusion
  76.3 5.1 %fusion.3 = bf16[1,1536,1408]{2,1,0:T(8,128)(2,1)} fusion(bf16[256,1,1408]{2,0,1:T(8,128)(2,1)} %copy-done.4, f32[256,1536]{1,0:T(8,128)} %copy-done.14), kind=kOutput, calls=%fused_computation.10 | convolution fusion | flops 1111425024 | bytes 6619136 | tf_op jit(solution)/shard_map/dot_general | solution.py:62
  81.4 35.2 %reduce-scatter.2.cloned.1.call-done = f32[64,2816]{1,0:T(8,128)} async-done(((f32[256,2816]{1,0:T(8,128)}), f32[64,2816]{1,0:T(8,128)}) %reduce-scatter.2.cloned.1.call-update) | async-done | bytes 720912 | tf_op jit(solution)/shard_map/reduce_scatter | solution.py:72
  116.7 1.1 convert.4
  119.9 7.1 %all-to-all-start.2 = ((bf16[32,2,1408]{2,1,0:T(2,128)(2,1)}), bf16[32,2,1408]{2,1,0:T(2,128)(2,1)S(1)}, u32[]{:S(2)}, u32[]{:S(2)}) async-start(bf16[32,2,1408]{2,1,0:T(2,128)(2,1)} %reshape.51), calls=%async_computation.3 | async-start | bytes 360448 | tf_op jit(solution)/shard_map/all_to_all | solution.py:79
  127.0 4.7 %fusion.2 = bf16[1,1408,1536]{2,1,0:T(8,128)(2,1)} fusion(bf16[256,1536]{1,0:T(8,128)(2,1)} %copy-done.15, bf16[256,1,1408]{2,0,1:T(8,128)(2,1)} %all_gather.6), kind=kOutput, calls=%fused_computation.9 | convolution fusion | flops 1109458944 | bytes 5832704 | tf_op jit(solution)/shard_map/dot_general | solution.py:65
  133.2 1.5 all-to-all-done.2
  134.7 6.2 %all-to-all-start.3 = ((bf16[32,2,1408]{2,1,0:T(2,128)(2,1)}), bf16[32,2,1408]{2,1,0:T(2,128)(2,1)}, u32[]{:S(2)}, u32[]{:S(2)}) async-start(bf16[32,2,1408]{2,1,0:T(2,128)(2,1)} %reshape.53), calls=%async_computation.4 | async-start | bytes 360448 | tf_op jit(solution)/shard_map/all_to_all | solution.py:78
  141.1 1.0 reduce.2
  142.2 2.7 convolution_bitcast_fusion.1
  145.7 3.0 all-to-all-done.3
  148.7 1.5 reshape.54
  150.2 1.7 reduce.3
  153.0 1.6 convolution_bitcast_fusion
  154.6 3.6 %fusion.30 = f32[1408,32]{0,1:T(8,128)} fusion(bf16[2,512,1408]{2,1,0:T(8,128)(2,1)} %param.6, f32[2,512]{1,0:T(2,128)S(1)} %copy-done.9, f32[2,512,32]{1,2,0:T(8,128)} %fusion.47, f32[2,512,32]{1,2,0:T(8,128)} %fusion.68, f32[2,512,32]{1,2,0:T(8,128)} %convolution_bitcast_fusion, f32[]{:T(128)} %bitcast.84), kind=kOutput, calls=%fused_computation.33 | convolution fusion | flops 96810016 | bytes 3461124 | tf_op jit(solution)/shard_map/btd,bts->ds/dot_general | solution.py:92
  158.2 5.6 %fusion.8 = (f32[2,512]{1,0:T(2,128)S(1)}, f32[2,512,1408]{2,1,0:T(8,128)}) fusion(bf16[2,512,1408]{2,1,0:T(8,128)(2,1)} %param.6, f32[]{:T(128)} %bitcast.85, f32[32]{0:T(128)S(1)} %copy-done.13, bf16[1408,32]{0,1:T(8,128)(2,1)S(1)} %copy-done.3, f32[2,512,32]{1,2,0:T(8,128)S(1)} %copy-done.5, f32[2,512,32]{1,2,0:T(8,128)} %fusion.68, ...), kind=kOutput, calls=%fused_computation.15 | convolution fusion | flops 98340896 | bytes 9138308 | tf_op jit(solution)/shard_map/bts,ds->btd/dot_general | solution.py:89
  163.8 5.6 %fusion.5 = bf16[2,512,1408]{2,1,0:T(8,128)(2,1)} fusion(bf16[2,512,1408]{2,1,0:T(8,128)(2,1)} %param.6, f32[2,512,1408]{2,1,0:T(8,128)} %get-tuple-element.9, f32[2,512]{1,0:T(2,128)S(1)} %multiply_multiply_fusion.1, f32[]{:T(128)} %bitcast.83, f32[2,512]{1,0:T(2,128)S(1)} %copy-done.9, bf16[32,2,1,1408]{3,1,0,2:T(2,128)(2,1)S(1)} %all_to_all.61, ...), kind=kOutput, calls=%fused_computation.12 | convolution fusion | flops 103841792 | bytes 11853828 | tf_op jit(solution)/shard_map/bts,bsd->btd/dot_general | solution.py:83
  169.4 130.2 %all-reduce.2.cloned.1.call-done = f32[1408,32]{0,1:T(8,128)} async-done(((f32[1408,32]{0,1:T(8,128)}), f32[1408,32]{0,1:T(8,128)}) %all-reduce.2.cloned.1.call-update) | async-done | bytes 180240 | tf_op jit(solution)/shard_map/psum | solution.py:98
  299.6 1.5 multiply_reduce_fusion.4
  302.5 1.4 add_add_fusion.1
  (69 shorter events, 12.3 us)
Async XLA Ops:
  7.2 16.9 %copy-start = (bf16[2,512,1408]{2,1,0:T(8,128)(2,1)S(1)}, bf16[2,512,1408]{2,1,0:T(8,128)(2,1)}, u32[]{:S(2)}) copy-start(bf16[2,512,1408]{2,1,0:T(8,128)(2,1)} %param.11) | copy-start | bytes 8650756
  7.2 4.9 %copy-start.1 = (bf16[2,512,1408]{2,1,0:T(8,128)(2,1)S(1)}, bf16[2,512,1408]{2,1,0:T(8,128)(2,1)}, u32[]{:S(2)}) copy-start(bf16[2,512,1408]{2,1,0:T(8,128)(2,1)} %param.6) | copy-start | bytes 8650756
  7.2 4.9 %copy-start.2 = (bf16[1408,32]{0,1:T(8,128)(2,1)S(1)}, bf16[1408,32]{0,1:T(8,128)(2,1)}, u32[]{:S(2)}) copy-start(bf16[1408,32]{0,1:T(8,128)(2,1)} %param.7) | copy-start | bytes 270340
  9.8 1.7 copy-start.6
  9.8 1.7 copy-start.8
  11.5 0.5 copy-start.12
  13.2 0.8 copy-start.10
  14.8 17.1 %all-to-all-start = ((bf16[2,32,1408]{2,0,1:T(2,128)(2,1)}), bf16[2,32,1408]{2,0,1:T(2,128)(2,1)S(1)}, u32[]{:S(2)}, u32[]{:S(2)}) async-start(bf16[2,32,1408]{2,0,1:T(2,128)(2,1)} %copy.20), calls=%async_computation | async-start | bytes 360448 | tf_op jit(solution)/shard_map/all_to_all | solution.py:45
  31.9 18.7 %all-to-all-start.1 = ((bf16[2,32,1408]{2,0,1:T(2,128)(2,1)}), bf16[2,32,1408]{2,0,1:T(2,128)(2,1)}, u32[]{:S(2)}, u32[]{:S(2)}) async-start(bf16[2,32,1408]{2,0,1:T(2,128)(2,1)} %copy.21), calls=%async_computation.1 | async-start | bytes 360448 | tf_op jit(solution)/shard_map/all_to_all | solution.py:46
  36.5 80.2 %reduce-scatter.2.cloned.1.call-start = ((), (), s32[]{:S(2)}) async-start(), calls=%async_computation.5 | async-start | bytes 3604480 | tf_op jit(solution)/shard_map/reduce_scatter | solution.py:72
  61.5 8.4 %copy-start.4 = (bf16[256,1,1408]{2,0,1:T(8,128)(2,1)}, bf16[256,1,1408]{2,0,1:T(8,128)(2,1)S(1)}, u32[]{:S(2)}) copy-start(bf16[256,1,1408]{2,0,1:T(8,128)(2,1)S(1)} %all_gather.7) | copy-start | bytes 2162692
  61.5 8.4 %slice-start = ((s8[4325376]{0:T(1024)(128)(4,1)}), s8[4194304]{0:T(1024)(128)(4,1)S(1)}, s32[]{:S(2)}) async-start(s8[4325376]{0:T(1024)(128)(4,1)} %bitcast.87), calls=%async_computation.7 | async-start | bytes 8388608
  65.6 4.3 %copy-start.14 = (f32[256,1536]{1,0:T(8,128)}, f32[256,1536]{1,0:T(8,128)S(1)}, u32[]{:S(2)}) copy-start(f32[256,1536]{1,0:T(8,128)S(1)} %fusion.15) | copy-start | bytes 4718596
  65.6 4.3 %slice-start.1 = ((s8[4325376]{0:T(1024)(128)(4,1)}), s8[131072]{0:T(1024)(128)(4,1)S(1)}, s32[]{:S(2)}) async-start(s8[4325376]{0:T(1024)(128)(4,1)} %bitcast.87), calls=%async_computation.8 | async-start | bytes 262144
  65.6 5.9 %slice-start.2 = ((s8[4325376]{0:T(1024)(128)(4,1)}), s8[4194304]{0:T(1024)(128)(4,1)S(1)}, s32[]{:S(2)}) async-start(s8[4325376]{0:T(1024)(128)(4,1)} %bitcast.89), calls=%async_computation.9 | async-start | bytes 8388608
  69.9 1.6 slice-start.3
  71.5 1.4 copy-start.15
  74.7 0.9 copy-start.11
  119.9 14.7 %all-to-all-start.2 = ((bf16[32,2,1408]{2,1,0:T(2,128)(2,1)}), bf16[32,2,1408]{2,1,0:T(2,128)(2,1)S(1)}, u32[]{:S(2)}, u32[]{:S(2)}) async-start(bf16[32,2,1408]{2,1,0:T(2,128)(2,1)} %reshape.51), calls=%async_computation.3 | async-start | bytes 360448 | tf_op jit(solution)/shard_map/all_to_all | solution.py:79
  134.7 14.0 %all-to-all-start.3 = ((bf16[32,2,1408]{2,1,0:T(2,128)(2,1)}), bf16[32,2,1408]{2,1,0:T(2,128)(2,1)}, u32[]{:S(2)}, u32[]{:S(2)}) async-start(bf16[32,2,1408]{2,1,0:T(2,128)(2,1)} %reshape.53), calls=%async_computation.4 | async-start | bytes 360448 | tf_op jit(solution)/shard_map/all_to_all | solution.py:78
  140.9 158.8 %all-reduce.2.cloned.1.call-start = ((), (), s32[]{:S(2)}) async-start(), calls=%async_computation.6 | async-start | bytes 360448 | tf_op jit(solution)/shard_map/psum | solution.py:98
  151.9 2.6 copy-start.9
  152.9 5.3 %copy-start.3 = (bf16[1408,32]{0,1:T(8,128)(2,1)S(1)}, bf16[1408,32]{0,1:T(8,128)(2,1)}, u32[]{:S(2)}) copy-start(bf16[1408,32]{0,1:T(8,128)(2,1)} %param.7) | copy-start | bytes 270340
  152.9 5.3 %copy-start.13 = (f32[32]{0:T(128)S(1)}, f32[32]{0:T(128)}, u32[]{:S(2)}) copy-start(f32[32]{0:T(128)} %copy-done.12) | copy-start | bytes 388
  154.6 3.6 %copy-start.5 = (f32[2,512,32]{1,2,0:T(8,128)S(1)}, f32[2,512,32]{1,2,0:T(8,128)}, u32[]{:S(2)}) copy-start(f32[2,512,32]{1,2,0:T(8,128)} %fusion.47) | copy-start | bytes 393220
  158.2 5.6 %copy-start.7 = (f32[2,512]{1,0:T(2,128)S(1)}, f32[2,512]{1,0:T(2,128)}, u32[]{:S(2)}) copy-start(f32[2,512]{1,0:T(2,128)} %copy-done.6) | copy-start | bytes 12292
Sparse Core Ops, SparseCore 0:
  74.9 41.7 reduce-scatter.1
  158.3 141.2 all-reduce.1
where the time goes:
time: 312 us; the launch traced here: 311 us
  waiting for transfers between devices  175 us (56%)
  matrix products  43.5 us (14%)
  starting transfers between devices  27.2 us (9%)
  blocking collectives  23.9 us (8%)
  between operations  16.5 us (5%)
  other arithmetic  16 us (5%)
  local copies, waits for them, and re-layouts  8.27 us (3%)
    psum x1, waiting for transfers between devices, body(): keys_total = lax.psum(keys_local, ('dp', 'expert'))  130 us
    reduce_scatter x1, waiting for transfers between devices, body(): lax.psum_scatter(jnp.concatenate([out_term, back_term], axis=1), 'dp', sc...  35.2 us
    all_gather x1, blocking collectives, body(): lax.all_gather(sent_in, 'dp', axis=0, tiled=True)  14 us
    all_gather x1, blocking collectives, body(): lax.all_gather(sent_grad, 'dp', axis=0, tiled=True)  9.87 us
    all_to_all x1, starting transfers between devices, body(): lax.all_to_all(slot_in, 'expert', split_axis=1, concat_axis=0, tiled=True)  9.23 us
    all_to_all x1, starting transfers between devices, body(): lax.all_to_all(back_rows, 'expert', split_axis=0, concat_axis=1, tiled=True)  7.07 us
  transfers between devices with their start and end apart: 6, of which 5 were waited for; matrix products, arithmetic and copies ran while one was open for 10% of the time, Pallas kernels for 0%

commit v1 on v0

v1 whole, which is shorter than its diff:
```python
import functools
import math

import jax
import jax.numpy as jnp
from jax import lax
from jax.experimental import pallas as pl
from jax.experimental.pallas import tpu as pltpu
from jax.sharding import PartitionSpec as P

EPS = 1e-06
MESH = pl.DeviceIdType.MESH
F32 = jnp.float32
BF16 = jnp.bfloat16
NN = (((1,), (0,)), ((), ()))
NT = (((1,), (1,)), ((), ()))
TN = (((0,), (0,)), ((), ()))


def dot(a, b, dims=NN):
    return lax.dot_general(a, b, dims, preferred_element_type=F32)


def selector(rows, cols, stride, offset):
    i = lax.broadcasted_iota(jnp.int32, (rows, cols), 0)
    j = lax.broadcasted_iota(jnp.int32, (rows, cols), 1)
    return jnp.where(i == j * stride + offset, 1.0, 0.0).astype(BF16)


def wait_for(ref, sem):
    pltpu.make_async_copy(ref, ref, sem).wait()


def slot_kernel(
    sizes,
    tok_h, cot_h, w1_h, w2_h, keys_ref, scale_ref,
    gt_o, gi_o, go_o, gk_o,
    tok, cot, w1, w2, at, mix_b, mix_c,
    kt, keysn, normed, rinv_s, logit_s, disp_s, comb_s, mix_in, mix_grad,
    send_in, send_grad, recv_in, recv_grad,
    x, gs, act, slope, pg, xt, actt,
    own_out, own_back, pair_out, pair_back, pair_out_r, pair_back_r,
    send_out, send_bk, recv_out, recv_bk, rows_out, rows_bk,
    key_send, key_recv, key_tot,
    load_sem, send_sem, recv_sem, in_sem, twin_sem, part_sem,
):
    images, tokens, width, experts, hidden, ny, nx, nz = sizes
    layer = 2 * nx * nz
    near = ny * layer
    half = near * images
    scale = scale_ref[0]
    dp = lax.axis_index("dp")
    ex = lax.axis_index("expert")
    zh, core = dp // 2, dp % 2
    px, py = (ex // nz) % nx, ex // (nz * nx)
    pz = zh * nz + ex % nz
    me = (py * nx + px) * 2 * nz + pz
    twin = {"dp": zh * 2 + 1 - core, "expert": ex}

    zs = [(pz + d) % (2 * nz) for d in range(2 * nz)]
    xs = [(px + d) % nx for d in range(nx)]
    ys = [(py + d) % ny * nx for d in range(ny)]
    z_dp = [z // nz * 2 + core for z in zs]
    z_ex = [z % nz for z in zs]

    def source(group):
        return ys[(ny - group) % ny] * 2 * nz

    def each_partner(body):
        for group in range(ny):
            for dx in range(nx):
                plane = ys[group] + xs[dx]
                for dz in range(2 * nz):
                    if group or dx or dz:
                        ee = plane * nz + z_ex[dz]
                        device = {"dp": z_dp[dz], "expert": ee}
                        body(group, plane * 2 * nz + zs[dz], ee, device)

    def load(index, src, dst):
        return pltpu.make_async_copy(src, dst, load_sem.at[index])

    loads = [load(b, tok_h.at[b], tok.at[pl.ds(b * tokens, tokens)]) for b in range(images)]
    loads += [
        load(images + b, cot_h.at[b], cot.at[pl.ds(b * tokens, tokens)]) for b in range(images)
    ]
    loads += [load(2 * images, w1_h.at[0], w1), load(2 * images + 1, w2_h.at[0], w2)]
    for one in loads[: 2 * images]:
        one.start()

    barrier = pltpu.get_barrier_semaphore()

    def greet(group, index, ee, device):
        pl.semaphore_signal(barrier, inc=1, device_id=device, device_id_type=MESH)

    each_partner(greet)
    for far in (zh, 1 - zh):
        pl.semaphore_signal(
            barrier, inc=1, device_id={"dp": far * 2 + 1 - core, "expert": ex}, device_id_type=MESH
        )

    key_rows = keys_ref[...].astype(F32)
    kt[...] = key_rows
    keysn[...] = (
        key_rows * lax.rsqrt(jnp.sum(key_rows * key_rows, axis=1, keepdims=True) + EPS)
    ).astype(BF16)

    for b in range(images):
        loads[b].wait()
        if b == 0:
            loads[2 * images].start()
            loads[2 * images + 1].start()
        rows = pl.ds(b * tokens, tokens)
        for i in range(tokens // 128):
            part = tok[b * tokens + i * 128 : b * tokens + (i + 1) * 128, :].astype(F32)
            square = part * part
            acc = square[:, :128]
            for j in range(1, width // 128):
                acc = acc + square[:, j * 128 : (j + 1) * 128]
            rinv_s[b, :, i * 128 : (i + 1) * 128] = lax.rsqrt(
                jnp.sum(acc.T, axis=0, keepdims=True) + EPS
            )
            down = lax.rsqrt(jnp.sum(acc, axis=1, keepdims=True) + EPS)
            normed[i * 128 : (i + 1) * 128, :] = (part * down).astype(BF16)
        logits = dot(keysn[...], normed[...], NT) * scale
        expo = jnp.exp(logits)
        disp = expo / jnp.sum(expo, axis=1, keepdims=True)
        comb = expo / jnp.sum(expo, axis=0, keepdims=True)
        logit_s[b] = logits
        disp_s[b] = disp
        comb_s[b] = comb
        disp_b = disp.astype(BF16)
        at[b, experts:, :] = disp_b
        spread = selector(images * experts, experts, images, b)
        mix_in[:, rows] = dot(spread, disp_b).astype(BF16)
        mix_grad[:, rows] = dot(spread, comb.astype(BF16)).astype(BF16)

    def remote(src, dst, send, recv, device):
        return pltpu.make_async_remote_copy(
            src_ref=src, dst_ref=dst, send_sem=send, recv_sem=recv,
            device_id=device, device_id_type=MESH,
        )

    def pack(rows_ref, start, blocks_ref, first, count):
        for i in range(count):
            rows_ref[start + i * images : start + (i + 1) * images, :] = blocks_ref[first + i]

    def out_of_experts(kind, out_ref, in_ref):
        def one(group, index, ee, device):
            remote(
                out_ref.at[ee], in_ref.at[me], send_sem.at[kind], in_sem.at[kind, group], device
            ).start()

        each_partner(one)
        in_ref[me] = out_ref[ex]

    def unpack(blocks_ref, value):
        for i in range(experts):
            blocks_ref[i] = value[i * images : (i + 1) * images, :]

    unpack(send_in, dot(mix_in[...], tok[...]).astype(BF16))
    pl.semaphore_wait(barrier, near + 1)
    out_of_experts(0, send_in, recv_in)
    for b in range(images):
        loads[images + b].wait()
    unpack(send_grad, dot(mix_grad[...], cot[...]).astype(BF16))
    out_of_experts(1, send_grad, recv_grad)

    def arrive(kind, in_ref, rows_ref):
        copies = []
        for group in range(ny):
            count = layer if group else layer - 1
            wait_for(in_ref.at[pl.ds(0, count)], in_sem.at[kind, group])
            pack(rows_ref, group * layer * images, in_ref, source(group), layer)
            mine = pl.ds(group * layer * images, layer * images)
            theirs = pl.ds(half + group * layer * images, layer * images)
            copies.append(
                remote(
                    rows_ref.at[mine], rows_ref.at[theirs],
                    part_sem.at[kind, group], twin_sem.at[kind, group], twin,
                )
            )
            copies[-1].start()
        return copies

    copies_in = arrive(0, recv_in, x)
    loads[2 * images].wait()
    loads[2 * images + 1].wait()
    for one in copies_in:
        one.wait_recv()

    step = min(256, hidden)

    def first(j, carry):
        cols = pl.ds(pl.multiple_of(j * step, step), step)
        pre = dot(x[...], w1[:, cols])
        cdf = 0.5 * (1.0 + lax.erf(pre * 0.7071067811865476))
        act[:, cols] = (pre * cdf).astype(BF16)
        slope[:, cols] = cdf + pre * jnp.exp(-0.5 * pre * pre) * 0.3989422804014327
        return carry

    lax.fori_loop(0, hidden // step, first, 0, unroll=2)

    wide = min(256, width)
    parts = -(-width // wide)

    def columns(j):
        return pl.ds(pl.multiple_of(jnp.minimum(j * wide, width - wide), 128), wide)

    def pair_copy(kind, j, src, dst):
        return remote(src.at[j], dst.at[j], send_sem.at[4 + kind], recv_sem.at[4 + kind], twin)

    def second(j, carry):
        res = dot(act[...], w2[:, columns(j)])
        pair_out[j] = res[half:].astype(BF16)
        pair_copy(0, j, pair_out, pair_out_r).start()
        own_out[j] = res[:half]
        return carry

    lax.fori_loop(0, parts, second, 0)

    copies_grad = arrive(1, recv_grad, gs)
    for one in copies_grad:
        one.wait_recv()

    def third(j, carry):
        cols = pl.ds(pl.multiple_of(j * step, step), step)
        pg[:, cols] = (dot(gs[...], w2[cols, :], NT) * slope[:, cols]).astype(BF16)
        return carry

    def chip_sums(kind, own, pair_r, rows_ref, out_ref, in_ref):
        wait_for(pair_r, recv_sem.at[4 + kind])
        for j in range(parts):
            start = min(j * wide, width - wide)
            rows_ref[:, start : start + wide] = (own[j] + pair_r[j].astype(F32)).astype(BF16)
        for group in range(ny):
            for i in range(layer):
                row = (group * layer + i) * images
                out_ref[source(group) + i] = rows_ref[row : row + images, :]

        def one(group, index, ee, device):
            remote(
                out_ref.at[index], in_ref.at[me], send_sem.at[2 + kind], in_sem.at[2 + kind, group],
                device,
            ).start()

        each_partner(one)
        in_ref[me] = out_ref[me]

    chip_sums(0, own_out, pair_out_r, rows_out, send_out, recv_out)
    lax.fori_loop(0, hidden // step, third, 0, unroll=2)

    def fourth(j, carry):
        res = dot(pg[...], w1[columns(j), :], NT)
        pair_back[j] = res[half:].astype(BF16)
        pair_copy(1, j, pair_back, pair_back_r).start()
        own_back[j] = res[:half]
        return carry

    lax.fori_loop(0, parts, fourth, 0)
    chip_sums(1, own_back, pair_back_r, rows_bk, send_bk, recv_bk)

    def turn(src, dst, size):
        same = selector(wide, wide, 1, 0)

        def one(j, carry):
            cols = pl.ds(pl.multiple_of(jnp.minimum(j * wide, size - wide), 128), wide)
            dst[cols, :] = dot(same, src[:, cols], NT).astype(BF16)
            return carry

        lax.fori_loop(0, -(-size // wide), one, 0)

    def product(left, right, out, size):
        def one(j, carry):
            rows = pl.ds(pl.multiple_of(j * size, 16), size)
            out[0, rows, :] = dot(left[rows, :], right[...]).astype(BF16)
            return carry

        lax.fori_loop(0, left.shape[0] // size, one, 0)

    turn(act, actt, hidden)
    product(actt, gs, go_o, hidden // 4)
    turn(x, xt, width)
    product(xt, pg, gi_o, width // 4)

    def collect(kind, in_ref, rows_ref):
        for group in range(ny):
            count = layer if group else layer - 1
            wait_for(in_ref.at[pl.ds(0, count)], in_sem.at[2 + kind, group])
            pack(rows_ref, group * layer * images, in_ref, source(group), layer)

    def gathered(rows_ref, b):
        i = lax.broadcasted_iota(jnp.int32, (experts, half), 0)
        j = lax.broadcasted_iota(jnp.int32, (experts, half), 1)
        slot = j // images
        group = slot // layer
        plane = (py + ny - group) % ny * nx + slot % layer // (2 * nz)
        wanted = (j % images == b) & (plane * nz + slot % nz == i)
        return dot(jnp.where(wanted, 1.0, 0.0).astype(BF16), rows_ref[...]).astype(BF16)

    collect(0, recv_out, rows_out)
    parts_lg = []
    for b in range(images):
        rows = pl.ds(b * tokens, tokens)
        comb_grad = dot(gathered(rows_out, b), cot[rows, :], NT)
        comb = comb_s[b]
        parts_lg.append(comb * (comb_grad - jnp.sum(comb * comb_grad, axis=0, keepdims=True)))

    collect(1, recv_bk, rows_bk)
    keys_grad = None
    for b in range(images):
        rows = pl.ds(b * tokens, tokens)
        back = gathered(rows_bk, b)
        mix_b[b, :experts, :] = keysn[...]
        mix_b[b, experts:, :] = back
        disp_grad = dot(back, tok[rows, :], NT)
        disp = disp_s[b]
        lg = parts_lg[b] + disp * (disp_grad - jnp.sum(disp * disp_grad, axis=1, keepdims=True))
        rinv = rinv_s[b]
        scaled = (lg * (scale * rinv)).astype(BF16)
        at[b, :experts, :] = scaled
        mix_c[b] = rinv * rinv * jnp.sum(lg * logit_s[b], axis=0, keepdims=True)
        term = dot(scaled, tok[rows, :])
        keys_grad = term if keys_grad is None else keys_grad + term

    for e in range(experts):
        key_send[e] = keys_grad[e : e + 1, :]

    for dy in range(ny):
        for dx in range(nx):
            for dz in range(nz):
                if dy or dx or dz:
                    ee = (ys[dy] + xs[dx]) * nz + z_ex[dz]
                    remote(
                        key_send.at[ee], key_recv.at[ex], send_sem.at[6], recv_sem.at[6],
                        {"dp": dp, "expert": ee},
                    ).start()
    key_recv[ex] = key_send[ex]
    most = pl.ds(0, experts - 1)

    per = min(256, tokens)
    for b in range(images):

        def one(j, carry, b=b):
            cut = pl.ds(pl.multiple_of(j * per, per), per)
            rows = pl.ds(pl.multiple_of(b * tokens + j * per, per), per)
            res = dot(at[b, :, cut], mix_b[b], TN)
            col = jnp.broadcast_to(mix_c[b, :, cut], (128, per)).T
            for k in range(width // 128):
                cols = slice(k * 128, (k + 1) * 128)
                gt_o[b, cut, cols] = (res[:, cols] - tok[rows, cols].astype(F32) * col).astype(BF16)
            return carry

        lax.fori_loop(0, tokens // per, one, 0)

    wait_for(key_recv.at[most], recv_sem.at[6])
    total = key_recv[0]
    for e in range(1, experts):
        total = total + key_recv[e]
    key_tot[dp] = total
    for k in range(1, 4):
        remote(
            key_tot.at[dp], key_tot.at[dp], send_sem.at[7], recv_sem.at[7],
            {"dp": (dp + k) % 4, "expert": ex},
        ).start()
    wait_for(key_tot.at[pl.ds(0, 3)], recv_sem.at[7])
    grad = (key_tot[0] + key_tot[1]) + (key_tot[2] + key_tot[3])
    own = kt[pl.ds(ex, 1), :]
    r = lax.rsqrt(jnp.sum(own * own, axis=1, keepdims=True) + EPS)
    gk_o[...] = grad * r - own * (r * r * r * jnp.sum(grad * own, axis=1, keepdims=True))

    some = pl.ds(0, near - 1)
    for kind, ref in enumerate((recv_in, recv_grad, recv_out, recv_bk)):
        wait_for(ref.at[some], send_sem.at[kind])
    wait_for(pair_out, send_sem.at[4])
    wait_for(pair_back, send_sem.at[5])
    for one in copies_in + copies_grad:
        one.wait_send()
    wait_for(key_recv.at[most], send_sem.at[6])
    wait_for(key_tot.at[pl.ds(0, 3)], send_sem.at[7])


def slots(sizes, tokens, cotangents, w_in, w_out, keys, scale):
    images, toks, width, experts, hidden, ny, nx, nz = sizes
    near = 2 * experts
    rows = near * images * 2
    half = near * images
    wide = min(256, width)
    parts = -(-width // wide)
    vmem = pltpu.VMEM
    dma = pltpu.SemaphoreType.DMA
    any_space = pl.BlockSpec(memory_space=pl.ANY)
    local = pl.BlockSpec(memory_space=pltpu.VMEM)
    flops = 2 * rows * width * hidden * 4
    return pl.pallas_call(
        functools.partial(slot_kernel, sizes),
        out_shape=(
            vmem((images, toks, width), BF16),
            vmem((1, width, hidden), BF16),
            vmem((1, hidden, width), BF16),
            vmem((1, width), F32),
        ),
        in_specs=[any_space] * 4 + [local, pl.BlockSpec(memory_space=pltpu.SMEM)],
        out_specs=(local,) * 4,
        scratch_shapes=[
            vmem((images * toks, width), BF16),
            vmem((images * toks, width), BF16),
            vmem((width, hidden), BF16),
            vmem((hidden, width), BF16),
            vmem((images, 2 * experts, toks), BF16),
            vmem((images, 2 * experts, width), BF16),
            vmem((images, 1, toks), F32),
            vmem((experts, width), F32),
            vmem((experts, width), BF16),
            vmem((toks, width), BF16),
            vmem((images, 1, toks), F32),
            vmem((images, experts, toks), F32),
            vmem((images, experts, toks), F32),
            vmem((images, experts, toks), F32),
            vmem((images * experts, images * toks), BF16),
            vmem((images * experts, images * toks), BF16),
            vmem((experts, images, width), BF16),
            vmem((experts, images, width), BF16),
            vmem((near, images, width), BF16),
            vmem((near, images, width), BF16),
            vmem((rows, width), BF16),
            vmem((rows, width), BF16),
            vmem((rows, hidden), BF16),
            vmem((rows, hidden), F32),
            vmem((rows, hidden), BF16),
            vmem((width, rows), BF16),
            vmem((hidden, rows), BF16),
            vmem((parts, half, wide), F32),
            vmem((parts, half, wide), F32),
            vmem((parts, half, wide), BF16),
            vmem((parts, half, wide), BF16),
            vmem((parts, half, wide), BF16),
            vmem((parts, half, wide), BF16),
            vmem((near, images, width), BF16),
            vmem((near, images, width), BF16),
            vmem((near, images, width), BF16),
            vmem((near, images, width), BF16),
            vmem((half, width), BF16),
            vmem((half, width), BF16),
            vmem((experts, 1, width), F32),
            vmem((experts, 1, width), F32),
            vmem((4, 1, width), F32),
            dma((2 * images + 2,)),
            dma((8,)),
            dma((8,)),
            dma((4, ny)),
            dma((2, ny)),
            dma((2, ny)),
        ],
        compiler_params=pltpu.CompilerParams(
            collective_id=0, has_side_effects=True, vmem_limit_bytes=44 * 1024 * 1024
        ),
        cost_estimate=pl.CostEstimate(
            flops=flops, bytes_accessed=4 * images * toks * width * 2, transcendentals=0
        ),
        name="slots",
    )(tokens, cotangents, w_in, w_out, keys, scale)


def store_kernel(gt, gi, go, gk, gt_h, gi_h, go_h, gk_h, sem):
    copies = []
    for src, dst in ((gi, gi_h), (go, go_h), (gt, gt_h), (gk, gk_h)):
        if len(src.shape) == 2:
            cuts = [(slice(None),)]
        elif src.shape[0] == 1:
            size = src.shape[1] // 4
            cuts = [(0, pl.ds(k * size, size)) for k in range(4)]
        else:
            cuts = [(k,) for k in range(src.shape[0])]
        for cut in cuts:
            copies.append(pltpu.make_async_copy(src.at[cut], dst.at[cut], sem.at[len(copies)]))
            copies[-1].start()
    for one in copies:
        one.wait()


def stored(*arrays):
    shape = jax.ShapeDtypeStruct
    return pl.pallas_call(
        store_kernel,
        out_shape=tuple(shape(one.shape, one.dtype) for one in arrays),
        in_specs=[pl.BlockSpec(memory_space=pltpu.VMEM)] * 4,
        out_specs=(pl.BlockSpec(memory_space=pl.ANY),) * 4,
        scratch_shapes=[pltpu.SemaphoreType.DMA((9 + arrays[0].shape[0],))],
        compiler_params=pltpu.CompilerParams(vmem_limit_bytes=4 * 1024 * 1024),
        cost_estimate=pl.CostEstimate(
            flops=0, bytes_accessed=2 * sum(one.size for one in arrays), transcendentals=0
        ),
        name="stored",
    )(*arrays)


def body(grid, tokens, slot_keys, logit_scale, w_in, w_out, grad_out):
    images, toks, width = tokens.shape
    sizes = (images, toks, width, slot_keys.shape[1], w_in.shape[2], *grid)
    gt, gi, go, gk = slots(sizes, tokens, grad_out, w_in, w_out, slot_keys.T, logit_scale)
    gt, gi, go, gk = stored(gt, gi, go, gk)
    return gt, gi, go, gk.reshape(width, 1)


def solution(mesh):
    experts = mesh.shape["expert"]
    nz = 2
    side = math.isqrt(experts // nz)
    grid = (experts // nz // side, side, nz)
    in_specs = (
        P(("dp", "expert"), None, None),
        P(),
        P(),
        P("expert", None, "dp"),
        P("expert", "dp", None),
        P(("dp", "expert"), None, None),
    )
    out_specs = (
        P(("dp", "expert"), None, None),
        P("expert", None, "dp"),
        P("expert", "dp", None),
        P(None, "expert"),
    )
    return jax.shard_map(
        functools.partial(body, grid),
        mesh=mesh,
        in_specs=in_specs,
        out_specs=out_specs,
        check_vma=False,
    )
```

time: 312 us -> 59.5 us (0.19)
  waiting for transfers between devices: 175 us -> 0 us
  Pallas kernels: 0 us -> 58 us
  matrix products: 43.5 us -> 0 us
  starting transfers between devices: 27.2 us -> 0 us
  blocking collectives: 23.9 us -> 0 us
  other arithmetic: 16 us -> 0 us
  between operations: 16.5 us -> 1.29 us
  local copies, waits for them, and re-layouts: 8.27 us -> 0 us
    psum x1 -> x0, waiting for transfers between devices: 130 us -> none  [body(): keys_total = lax.psum(keys_local, ('dp', 'expert'))]
    pallas_call x0 -> x2, Pallas kernels: none -> 58 us  [the longest x1 53.7 us: slots(): pl.pallas_call(functools.partial(slot_kernel, sizes), out_shape=(vmem((im...]
    dot_general x14 -> x0, matrix products: 43.5 us -> none  [the longest x1 5.6 us: body(): jnp.einsum('bts,bsd->btd', dispatch_b, slot_back, preferred_element_type=...]
    reduce_scatter x1 -> x0, waiting for transfers between devices: 35.2 us -> none  [body(): lax.psum_scatter(jnp.concatenate([out_term, back_term], axis=1), 'dp', sc...]
    all_to_all x4 -> x0, starting transfers between devices: 27.1 us -> none  [the longest x1 9.23 us: body(): lax.all_to_all(slot_in, 'expert', split_axis=1, concat_axis=0, tiled=True)]
    all_gather x2 -> x0, blocking collectives: 23.9 us -> none  [the longest x1 14 us: body(): lax.all_gather(sent_in, 'dp', axis=0, tiled=True)]
    all_to_all x4 -> x0, waiting for transfers between devices: 9.93 us -> none  [the longest x1 5.47 us: body(): lax.all_to_all(slot_in, 'expert', split_axis=1, concat_axis=0, tiled=True)]
    reduce_sum x3 -> x0, other arithmetic: 5.08 us -> none  [normalize(): return v * lax.rsqrt(jnp.sum(v * v, axis=axis, keepdims=True) + EPS)]
  transfers between devices with their start and end apart: 6 -> 0, of which waited for: 5 -> 0; matrix products, arithmetic and copies ran while one was open for 10% -> 0% of each run, Pallas kernels for 0% -> 0%
where the time goes in v1:
time: 59.5 us; the launch traced here: 59.3 us
  Pallas kernels  58 us (97%)
  between operations  1.29 us (2%)
    pallas_call x1, Pallas kernels, slots(): pl.pallas_call(functools.partial(slot_kernel, sizes), out_shape=(vmem((im...  53.7 us
    pallas_call x1, Pallas kernels, stored(): pl.pallas_call(store_kernel, out_shape=tuple((shape(one.shape, one.dtype)...  4.36 us

profile of v1, /device:TPU:1, one launch (start us, length us, event | category | flops | bytes accessed | tf_op | source)
XLA Modules:
  0.0 59.3 jit_solution(4544393669842720266)
XLA Ops:
  1.3 53.7 %slots.1 = (bf16[2,512,1408]{2,1,0:T(8,128)(2,1)S(1)}, bf16[1,1408,1536]{2,1,0:T(8,128)(2,1)S(1)}, bf16[1,1536,1408]{2,1,0:T(8,128)(2,1)S(1)}, f32[1,1408]{1,0:T(1,128)S(1)}) custom-call(bf16[2,512,1408]{2,1,0:T(8,128)(2,1)} %tok_h.1, bf16[2,512,1408]{2,1,0:T(8,128)(2,1)} %cot_h.1, bf16[1,1408,1536]{2,1,0:T(8,128)(2,1)} %w1_h.1, ...), custom_call_target="tpu_custom_call" | custom-call | flops 4429185024 | bytes 11534336 | tf_op jit(solution)/shard_map/slots/pallas_call | solution.py:394
  55.0 4.4 %stored.1 = (bf16[2,512,1408]{2,1,0:T(8,128)(2,1)}, bf16[1,1408,1536]{2,1,0:T(8,128)(2,1)}, bf16[1,1536,1408]{2,1,0:T(8,128)(2,1)}, f32[1,1408]{1,0:T(1,128)}) custom-call(bf16[2,512,1408]{2,1,0:T(8,128)(2,1)S(1)} %get-tuple-element.12.gt, bf16[1,1408,1536]{2,1,0:T(8,128)(2,1)S(1)} %get-tuple-element.13.gi, bf16[1,1536,1408]{2,1,0:T(8,128)(2,1)S(1)} %get-tuple-element.14.go, ...), custom_call_target="tpu_custom_call" | custom-call | bytes 11537152 | tf_op jit(solution)/shard_map/stored/pallas_call | solution.py:483

commit v2 on v1

--- a/solution.py
+++ b/solution.py
@@ -37,7 +37,7 @@
     gt_o, gi_o, go_o, gk_o,
     tok, cot, w1, w2, at, mix_b, mix_c,
     kt, keysn, normed, rinv_s, logit_s, disp_s, comb_s, mix_in, mix_grad,
-    send_in, send_grad, recv_in, recv_grad,
+    rows_first, send_in, send_grad, recv_in, recv_grad,
     x, gs, act, slope, pg, xt, actt,
     own_out, own_back, pair_out, pair_back, pair_out_r, pair_back_r,
     send_out, send_bk, recv_out, recv_bk, rows_out, rows_bk,
@@ -79,12 +79,23 @@
     def load(index, src, dst):
         return pltpu.make_async_copy(src, dst, load_sem.at[index])
 
-    loads = [load(b, tok_h.at[b], tok.at[pl.ds(b * tokens, tokens)]) for b in range(images)]
-    loads += [
-        load(images + b, cot_h.at[b], cot.at[pl.ds(b * tokens, tokens)]) for b in range(images)
+    pieces = 2
+    piece = tokens // pieces
+    tok_loads = [
+        load(
+            b * pieces + p, tok_h.at[b, pl.ds(p * piece, piece)],
+            tok.at[pl.ds(b * tokens + p * piece, piece)],
+        )
+        for b in range(images)
+        for p in range(pieces)
     ]
-    loads += [load(2 * images, w1_h.at[0], w1), load(2 * images + 1, w2_h.at[0], w2)]
-    for one in loads[: 2 * images]:
+    done = images * pieces
+    cot_loads = [
+        load(done + b, cot_h.at[b], cot.at[pl.ds(b * tokens, tokens)]) for b in range(images)
+    ]
+    done += images
+    weight_loads = [load(done, w1_h.at[0], w1), load(done + 1, w2_h.at[0], w2)]
+    for one in tok_loads:
         one.start()
 
     barrier = pltpu.get_barrier_semaphore()
@@ -105,22 +116,27 @@
     ).astype(BF16)
 
     for b in range(images):
-        loads[b].wait()
-        if b == 0:
-            loads[2 * images].start()
-            loads[2 * images + 1].start()
         rows = pl.ds(b * tokens, tokens)
-        for i in range(tokens // 128):
-            part = tok[b * tokens + i * 128 : b * tokens + (i + 1) * 128, :].astype(F32)
-            square = part * part
-            acc = square[:, :128]
-            for j in range(1, width // 128):
-                acc = acc + square[:, j * 128 : (j + 1) * 128]
-            rinv_s[b, :, i * 128 : (i + 1) * 128] = lax.rsqrt(
-                jnp.sum(acc.T, axis=0, keepdims=True) + EPS
-            )
-            down = lax.rsqrt(jnp.sum(acc, axis=1, keepdims=True) + EPS)
-            normed[i * 128 : (i + 1) * 128, :] = (part * down).astype(BF16)
+        for p in range(pieces):
+            tok_loads[b * pieces + p].wait()
+            if b == 0 and p == 0:
+                for one in (*cot_loads, *weight_loads):
+                    one.start()
+            for i in range(p * piece // 128, (p + 1) * piece // 128):
+                accs = []
+                for r in range(i * 128, (i + 1) * 128, 32):
+                    part = tok[b * tokens + r : b * tokens + r + 32, :].astype(F32)
+                    square = part * part
+                    acc = square[:, :128]
+                    for j in range(1, width // 128):
+                        acc = acc + square[:, j * 128 : (j + 1) * 128]
+                    accs.append(acc)
+                    down = lax.rsqrt(jnp.sum(acc, axis=1, keepdims=True) + EPS)
+                    normed[r : r + 32, :] = (part * down).astype(BF16)
+                acc = jnp.concatenate(accs, axis=0)
+                rinv_s[b, :, i * 128 : (i + 1) * 128] = lax.rsqrt(
+                    jnp.sum(acc.T, axis=0, keepdims=True) + EPS
+                )
         logits = dot(keysn[...], normed[...], NT) * scale
         expo = jnp.exp(logits)
         disp = expo / jnp.sum(expo, axis=1, keepdims=True)
@@ -129,7 +145,7 @@
         disp_s[b] = disp
         comb_s[b] = comb
         disp_b = disp.astype(BF16)
-        at[b, experts:, :] = disp_b
+        at[experts:, rows] = disp_b
         spread = selector(images * experts, experts, images, b)
         mix_in[:, rows] = dot(spread, disp_b).astype(BF16)
         mix_grad[:, rows] = dot(spread, comb.astype(BF16)).astype(BF16)
@@ -144,26 +160,33 @@
         for i in range(count):
             rows_ref[start + i * images : start + (i + 1) * images, :] = blocks_ref[first + i]
 
-    def out_of_experts(kind, out_ref, in_ref):
-        def one(group, index, ee, device):
-            remote(
-                out_ref.at[ee], in_ref.at[me], send_sem.at[kind], in_sem.at[kind, group], device
-            ).start()
-
-        each_partner(one)
+    def by_group(send):
+        todo = [[] for _ in range(ny)]
+        each_partner(lambda group, *rest: todo[group].append(rest))
+        for group in range(ny):
+            send(group, todo[group])
+
+    def out_of_experts(kind, value, out_ref, in_ref):
+        each = nx * nz
+        rows_first[...] = value
+
+        def send(group, devices):
+            part = rows_first[pl.ds(pl.multiple_of(ys[group] * nz * images, 16), each * images), :]
+            for i in range(each):
+                out_ref[ys[group] * nz + i] = part[i * images : (i + 1) * images, :]
+            for index, ee, device in devices:
+                remote(
+                    out_ref.at[ee], in_ref.at[me], send_sem.at[kind], in_sem.at[kind, group], device
+                ).start()
+
+        by_group(send)
         in_ref[me] = out_ref[ex]
 
-    def unpack(blocks_ref, value):
-        for i in range(experts):
-            blocks_ref[i] = value[i * images : (i + 1) * images, :]
-
-    unpack(send_in, dot(mix_in[...], tok[...]).astype(BF16))
     pl.semaphore_wait(barrier, near + 1)
-    out_of_experts(0, send_in, recv_in)
-    for b in range(images):
-        loads[images + b].wait()
-    unpack(send_grad, dot(mix_grad[...], cot[...]).astype(BF16))
-    out_of_experts(1, send_grad, recv_grad)
+    out_of_experts(0, dot(mix_in[...], tok[...]).astype(BF16), send_in, recv_in)
+    for one in cot_loads:
+        one.wait()
+    out_of_experts(1, dot(mix_grad[...], cot[...]).astype(BF16), send_grad, recv_grad)
 
     def arrive(kind, in_ref, rows_ref):
         copies = []
@@ -183,8 +206,8 @@
         return copies
 
     copies_in = arrive(0, recv_in, x)
-    loads[2 * images].wait()
-    loads[2 * images + 1].wait()
+    for one in weight_loads:
+        one.wait()
     for one in copies_in:
         one.wait_recv()
 
@@ -219,8 +242,6 @@
     lax.fori_loop(0, parts, second, 0)
 
     copies_grad = arrive(1, recv_grad, gs)
-    for one in copies_grad:
-        one.wait_recv()
 
     def third(j, carry):
         cols = pl.ds(pl.multiple_of(j * step, step), step)
@@ -232,21 +253,24 @@
         for j in range(parts):
             start = min(j * wide, width - wide)
             rows_ref[:, start : start + wide] = (own[j] + pair_r[j].astype(F32)).astype(BF16)
-        for group in range(ny):
+
+        def send(group, devices):
+            other = (ny - group) % ny
             for i in range(layer):
-                row = (group * layer + i) * images
-                out_ref[source(group) + i] = rows_ref[row : row + images, :]
-
-        def one(group, index, ee, device):
-            remote(
-                out_ref.at[index], in_ref.at[me], send_sem.at[2 + kind], in_sem.at[2 + kind, group],
-                device,
-            ).start()
-
-        each_partner(one)
+                row = (other * layer + i) * images
+                out_ref[source(other) + i] = rows_ref[row : row + images, :]
+            for index, ee, device in devices:
+                remote(
+                    out_ref.at[index], in_ref.at[me], send_sem.at[2 + kind],
+                    in_sem.at[2 + kind, group], device,
+                ).start()
+
+        by_group(send)
         in_ref[me] = out_ref[me]
 
     chip_sums(0, own_out, pair_out_r, rows_out, send_out, recv_out)
+    for one in copies_grad:
+        one.wait_recv()
     lax.fori_loop(0, hidden // step, third, 0, unroll=2)
 
     def fourth(j, carry):
@@ -257,8 +281,6 @@
         return carry
 
     lax.fori_loop(0, parts, fourth, 0)
-    chip_sums(1, own_back, pair_back_r, rows_bk, send_bk, recv_bk)
-
     def turn(src, dst, size):
         same = selector(wide, wide, 1, 0)
 
@@ -278,8 +300,9 @@
         lax.fori_loop(0, left.shape[0] // size, one, 0)
 
     turn(act, actt, hidden)
+    turn(x, xt, width)
+    chip_sums(1, own_back, pair_back_r, rows_bk, send_bk, recv_bk)
     product(actt, gs, go_o, hidden // 4)
-    turn(x, xt, width)
     product(xt, pg, gi_o, width // 4)
 
     def collect(kind, in_ref, rows_ref):
@@ -288,28 +311,29 @@
             wait_for(in_ref.at[pl.ds(0, count)], in_sem.at[2 + kind, group])
             pack(rows_ref, group * layer * images, in_ref, source(group), layer)
 
-    def gathered(rows_ref, b):
-        i = lax.broadcasted_iota(jnp.int32, (experts, half), 0)
-        j = lax.broadcasted_iota(jnp.int32, (experts, half), 1)
+    def gathered(rows_ref):
+        i = lax.broadcasted_iota(jnp.int32, (images * experts, half), 0)
+        j = lax.broadcasted_iota(jnp.int32, (images * experts, half), 1)
         slot = j // images
         group = slot // layer
         plane = (py + ny - group) % ny * nx + slot % layer // (2 * nz)
-        wanted = (j % images == b) & (plane * nz + slot % nz == i)
+        wanted = i == j % images * experts + plane * nz + slot % nz
         return dot(jnp.where(wanted, 1.0, 0.0).astype(BF16), rows_ref[...]).astype(BF16)
 
     collect(0, recv_out, rows_out)
+    slot_out = gathered(rows_out)
     parts_lg = []
     for b in range(images):
         rows = pl.ds(b * tokens, tokens)
-        comb_grad = dot(gathered(rows_out, b), cot[rows, :], NT)
+        comb_grad = dot(slot_out[b * experts : (b + 1) * experts], cot[rows, :], NT)
         comb = comb_s[b]
         parts_lg.append(comb * (comb_grad - jnp.sum(comb * comb_grad, axis=0, keepdims=True)))
 
     collect(1, recv_bk, rows_bk)
-    keys_grad = None
+    slot_back = gathered(rows_bk)
     for b in range(images):
         rows = pl.ds(b * tokens, tokens)
-        back = gathered(rows_bk, b)
+        back = slot_back[b * experts : (b + 1) * experts]
         mix_b[b, :experts, :] = keysn[...]
         mix_b[b, experts:, :] = back
         disp_grad = dot(back, tok[rows, :], NT)
@@ -317,10 +341,9 @@
         lg = parts_lg[b] + disp * (disp_grad - jnp.sum(disp * disp_grad, axis=1, keepdims=True))
         rinv = rinv_s[b]
         scaled = (lg * (scale * rinv)).astype(BF16)
-        at[b, :experts, :] = scaled
+        at[:experts, rows] = scaled
         mix_c[b] = rinv * rinv * jnp.sum(lg * logit_s[b], axis=0, keepdims=True)
-        term = dot(scaled, tok[rows, :])
-        keys_grad = term if keys_grad is None else keys_grad + term
+    keys_grad = dot(at[:experts, :], tok[...])
 
     for e in range(experts):
         key_send[e] = keys_grad[e : e + 1, :]
@@ -338,12 +361,12 @@
     most = pl.ds(0, experts - 1)
 
     per = min(256, tokens)
-    for b in range(images):
-
-        def one(j, carry, b=b):
+
+    def token_grads(b):
+        def one(j, carry):
             cut = pl.ds(pl.multiple_of(j * per, per), per)
             rows = pl.ds(pl.multiple_of(b * tokens + j * per, per), per)
-            res = dot(at[b, :, cut], mix_b[b], TN)
+            res = dot(at[:, rows], mix_b[b], TN)
             col = jnp.broadcast_to(mix_c[b, :, cut], (128, per)).T
             for k in range(width // 128):
                 cols = slice(k * 128, (k + 1) * 128)
@@ -352,6 +375,8 @@
 
         lax.fori_loop(0, tokens // per, one, 0)
 
+    for b in range(images // 2):
+        token_grads(b)
     wait_for(key_recv.at[most], recv_sem.at[6])
     total = key_recv[0]
     for e in range(1, experts):
@@ -362,6 +387,8 @@
             key_tot.at[dp], key_tot.at[dp], send_sem.at[7], recv_sem.at[7],
             {"dp": (dp + k) % 4, "expert": ex},
         ).start()
+    for b in range(images // 2, images):
+        token_grads(b)
     wait_for(key_tot.at[pl.ds(0, 3)], recv_sem.at[7])
     grad = (key_tot[0] + key_tot[1]) + (key_tot[2] + key_tot[3])
     own = kt[pl.ds(ex, 1), :]
@@ -406,7 +433,7 @@
             vmem((images * toks, width), BF16),
             vmem((width, hidden), BF16),
             vmem((hidden, width), BF16),
-            vmem((images, 2 * experts, toks), BF16),
+            vmem((2 * experts, images * toks), BF16),
             vmem((images, 2 * experts, width), BF16),
             vmem((images, 1, toks), F32),
             vmem((experts, width), F32),
@@ -418,6 +445,7 @@
             vmem((images, experts, toks), F32),
             vmem((images * experts, images * toks), BF16),
             vmem((images * experts, images * toks), BF16),
+            vmem((images * experts, width), BF16),
             vmem((experts, images, width), BF16),
             vmem((experts, images, width), BF16),
             vmem((near, images, width), BF16),
@@ -444,7 +472,7 @@
             vmem((experts, 1, width), F32),
             vmem((experts, 1, width), F32),
             vmem((4, 1, width), F32),
-            dma((2 * images + 2,)),
+            dma((3 * images + 2,)),
             dma((8,)),
             dma((8,)),
             dma((4, ny)),
@@ -467,10 +495,11 @@
         if len(src.shape) == 2:
             cuts = [(slice(None),)]
         elif src.shape[0] == 1:
-            size = src.shape[1] // 4
-            cuts = [(0, pl.ds(k * size, size)) for k in range(4)]
+            size = src.shape[1] // 8
+            cuts = [(0, pl.ds(k * size, size)) for k in range(8)]
         else:
-            cuts = [(k,) for k in range(src.shape[0])]
+            size = src.shape[1] // 2
+            cuts = [(k, pl.ds(j * size, size)) for k in range(src.shape[0]) for j in range(2)]
         for cut in cuts:
             copies.append(pltpu.make_async_copy(src.at[cut], dst.at[cut], sem.at[len(copies)]))
             copies[-1].start()
@@ -485,7 +514,7 @@
         out_shape=tuple(shape(one.shape, one.dtype) for one in arrays),
         in_specs=[pl.BlockSpec(memory_space=pltpu.VMEM)] * 4,
         out_specs=(pl.BlockSpec(memory_space=pl.ANY),) * 4,
-        scratch_shapes=[pltpu.SemaphoreType.DMA((9 + arrays[0].shape[0],))],
+        scratch_shapes=[pltpu.SemaphoreType.DMA((17 + 2 * arrays[0].shape[0],))],
         compiler_params=pltpu.CompilerParams(vmem_limit_bytes=4 * 1024 * 1024),
         cost_estimate=pl.CostEstimate(
             flops=0, bytes_accessed=2 * sum(one.size for one in arrays), transcendentals=0

time: 59.5 us -> 60.7 us (1.020)
  Pallas kernels: 58 us -> 59.2 us
    pallas_call x1, Pallas kernels: 53.7 us -> 54.8 us  [slots(): pl.pallas_call(functools.partial(slot_kernel, sizes), out_shape=(vmem((im...]
where the time goes in v2:
time: 60.7 us; the launch traced here: 60.5 us
  Pallas kernels  59.2 us (98%)
  between operations  1.29 us (2%)
    pallas_call x1, Pallas kernels, slots(): pl.pallas_call(functools.partial(slot_kernel, sizes), out_shape=(vmem((im...  54.8 us
    pallas_call x1, Pallas kernels, stored(): pl.pallas_call(store_kernel, out_shape=tuple((shape(one.shape, one.dtype)...  4.42 us

profile of v2, /device:TPU:1, one launch (start us, length us, event | category | flops | bytes accessed | tf_op | source)
XLA Modules:
  0.0 60.5 jit_solution(14479322459279921838)
XLA Ops:
  1.3 54.8 %slots.1 = (bf16[2,512,1408]{2,1,0:T(8,128)(2,1)S(1)}, bf16[1,1408,1536]{2,1,0:T(8,128)(2,1)S(1)}, bf16[1,1536,1408]{2,1,0:T(8,128)(2,1)S(1)}, f32[1,1408]{1,0:T(1,128)S(1)}) custom-call(bf16[2,512,1408]{2,1,0:T(8,128)(2,1)} %tok_h.1, bf16[2,512,1408]{2,1,0:T(8,128)(2,1)} %cot_h.1, bf16[1,1408,1536]{2,1,0:T(8,128)(2,1)} %w1_h.1, ...), custom_call_target="tpu_custom_call" | custom-call | flops 4429185024 | bytes 11534336 | tf_op jit(solution)/shard_map/slots/pallas_call | solution.py:421
  56.1 4.4 %stored.1 = (bf16[2,512,1408]{2,1,0:T(8,128)(2,1)}, bf16[1,1408,1536]{2,1,0:T(8,128)(2,1)}, bf16[1,1536,1408]{2,1,0:T(8,128)(2,1)}, f32[1,1408]{1,0:T(1,128)}) custom-call(bf16[2,512,1408]{2,1,0:T(8,128)(2,1)S(1)} %get-tuple-element.12.gt, bf16[1,1408,1536]{2,1,0:T(8,128)(2,1)S(1)} %get-tuple-element.13.gi, bf16[1,1536,1408]{2,1,0:T(8,128)(2,1)S(1)} %get-tuple-element.14.go, ...), custom_call_target="tpu_custom_call" | custom-call | bytes 11537152 | tf_op jit(solution)/shard_map/stored/pallas_call | solution.py:512

commit v3 on v1

--- a/solution.py
+++ b/solution.py
@@ -29,6 +29,33 @@
 
 def wait_for(ref, sem):
     pltpu.make_async_copy(ref, ref, sem).wait()
+
+
+def spread_offsets(dims):
+    left = [
+        (a, b, c) for a in range(dims[0]) for b in range(dims[1]) for c in range(dims[2])
+    ][1:]
+    share = {}
+    for one in left:
+        for kind in enumerate(one):
+            share[kind] = share.get(kind, 0) + 1
+    order, used, total = [(0, 0, 0)], dict.fromkeys(share, 0), len(left)
+    while left:
+        at = len(order)
+
+        def uneven(one):
+            taken = set(enumerate(one))
+            return sum(
+                (used[k] + (k in taken) - share[k] * at / total) ** 2 * (2 if k[1] else 1)
+                for k in share
+            )
+
+        best = min(left, key=lambda one: (round(uneven(one), 9), one))
+        left.remove(best)
+        order.append(best)
+        for kind in enumerate(best):
+            used[kind] += 1
+    return order
 
 
 def slot_kernel(
@@ -54,7 +81,6 @@
     zh, core = dp // 2, dp % 2
     px, py = (ex // nz) % nx, ex // (nz * nx)
     pz = zh * nz + ex % nz
-    me = (py * nx + px) * 2 * nz + pz
     twin = {"dp": zh * 2 + 1 - core, "expert": ex}
 
     zs = [(pz + d) % (2 * nz) for d in range(2 * nz)]
@@ -63,18 +89,17 @@
     z_dp = [z // nz * 2 + core for z in zs]
     z_ex = [z % nz for z in zs]
 
-    def source(group):
-        return ys[(ny - group) % ny] * 2 * nz
-
-    def each_partner(body):
-        for group in range(ny):
-            for dx in range(nx):
-                plane = ys[group] + xs[dx]
-                for dz in range(2 * nz):
-                    if group or dx or dz:
-                        ee = plane * nz + z_ex[dz]
-                        device = {"dp": z_dp[dz], "expert": ee}
-                        body(group, plane * 2 * nz + zs[dz], ee, device)
+    offsets = spread_offsets((ny, nx, 2 * nz))
+
+    def device_at(dy, dx, dz):
+        dz = dz % (2 * nz)
+        ee = (ys[dy % ny] + xs[dx % nx]) * nz + z_ex[dz]
+        return ee, {"dp": z_dp[dz], "expert": ee}
+
+    def each_partner(body, sign=1):
+        for p, (dy, dx, dz) in enumerate(offsets):
+            if p:
+                body(p, *device_at(sign * dy, sign * dx, sign * dz))
 
     def load(index, src, dst):
         return pltpu.make_async_copy(src, dst, load_sem.at[index])
@@ -89,7 +114,7 @@
 
     barrier = pltpu.get_barrier_semaphore()
 
-    def greet(group, index, ee, device):
+    def greet(p, ee, device):
         pl.semaphore_signal(barrier, inc=1, device_id=device, device_id_type=MESH)
 
     each_partner(greet)
@@ -145,13 +170,13 @@
             rows_ref[start + i * images : start + (i + 1) * images, :] = blocks_ref[first + i]
 
     def out_of_experts(kind, out_ref, in_ref):
-        def one(group, index, ee, device):
+        def one(p, ee, device):
             remote(
-                out_ref.at[ee], in_ref.at[me], send_sem.at[kind], in_sem.at[kind, group], device
+                out_ref.at[ee], in_ref.at[p], send_sem.at[kind], in_sem.at[kind, p // layer], device
             ).start()
 
         each_partner(one)
-        in_ref[me] = out_ref[ex]
+        in_ref[0] = out_ref[ex]
 
     def unpack(blocks_ref, value):
         for i in range(experts):
@@ -170,7 +195,7 @@
         for group in range(ny):
             count = layer if group else layer - 1
             wait_for(in_ref.at[pl.ds(0, count)], in_sem.at[kind, group])
-            pack(rows_ref, group * layer * images, in_ref, source(group), layer)
+            pack(rows_ref, group * layer * images, in_ref, group * layer, layer)
             mine = pl.ds(group * layer * images, layer * images)
             theirs = pl.ds(half + group * layer * images, layer * images)
             copies.append(
@@ -232,19 +257,17 @@
         for j in range(parts):
             start = min(j * wide, width - wide)
             rows_ref[:, start : start + wide] = (own[j] + pair_r[j].astype(F32)).astype(BF16)
-        for group in range(ny):
-            for i in range(layer):
-                row = (group * layer + i) * images
-                out_ref[source(group) + i] = rows_ref[row : row + images, :]
-
-        def one(group, index, ee, device):
+        for p in range(near):
+            out_ref[p] = rows_ref[p * images : (p + 1) * images, :]
+
+        def one(p, ee, device):
             remote(
-                out_ref.at[index], in_ref.at[me], send_sem.at[2 + kind], in_sem.at[2 + kind, group],
+                out_ref.at[p], in_ref.at[p], send_sem.at[2 + kind], in_sem.at[2 + kind, p // layer],
                 device,
             ).start()
 
-        each_partner(one)
-        in_ref[me] = out_ref[me]
+        each_partner(one, -1)
+        in_ref[0] = out_ref[0]
 
     chip_sums(0, own_out, pair_out_r, rows_out, send_out, recv_out)
     lax.fori_loop(0, hidden // step, third, 0, unroll=2)
@@ -286,30 +309,34 @@
         for group in range(ny):
             count = layer if group else layer - 1
             wait_for(in_ref.at[pl.ds(0, count)], in_sem.at[2 + kind, group])
-            pack(rows_ref, group * layer * images, in_ref, source(group), layer)
-
-    def gathered(rows_ref, b):
-        i = lax.broadcasted_iota(jnp.int32, (experts, half), 0)
-        j = lax.broadcasted_iota(jnp.int32, (experts, half), 1)
-        slot = j // images
-        group = slot // layer
-        plane = (py + ny - group) % ny * nx + slot % layer // (2 * nz)
-        wanted = (j % images == b) & (plane * nz + slot % nz == i)
-        return dot(jnp.where(wanted, 1.0, 0.0).astype(BF16), rows_ref[...]).astype(BF16)
+            pack(rows_ref, group * layer * images, in_ref, group * layer, layer)
+
+    i = lax.broadcasted_iota(jnp.int32, (images * experts, half), 0)
+    j = lax.broadcasted_iota(jnp.int32, (1, half), 1)
+    place = jnp.full((1, half), ex, jnp.int32)
+    for p, offset in enumerate(offsets):
+        place = jnp.where(j // images == p, device_at(*offset)[0], place)
+    wanted = i == place + j % images * experts
+    gather = jnp.where(wanted, 1.0, 0.0).astype(BF16)
+
+    def gathered(rows_ref):
+        return dot(gather, rows_ref[...]).astype(BF16)
 
     collect(0, recv_out, rows_out)
+    slot_out = gathered(rows_out)
     parts_lg = []
     for b in range(images):
         rows = pl.ds(b * tokens, tokens)
-        comb_grad = dot(gathered(rows_out, b), cot[rows, :], NT)
+        comb_grad = dot(slot_out[b * experts : (b + 1) * experts], cot[rows, :], NT)
         comb = comb_s[b]
         parts_lg.append(comb * (comb_grad - jnp.sum(comb * comb_grad, axis=0, keepdims=True)))
 
     collect(1, recv_bk, rows_bk)
+    slot_back = gathered(rows_bk)
     keys_grad = None
     for b in range(images):
         rows = pl.ds(b * tokens, tokens)
-        back = gathered(rows_bk, b)
+        back = slot_back[b * experts : (b + 1) * experts]
         mix_b[b, :experts, :] = keysn[...]
         mix_b[b, experts:, :] = back
         disp_grad = dot(back, tok[rows, :], NT)
@@ -325,15 +352,12 @@
     for e in range(experts):
         key_send[e] = keys_grad[e : e + 1, :]
 
-    for dy in range(ny):
-        for dx in range(nx):
-            for dz in range(nz):
-                if dy or dx or dz:
-                    ee = (ys[dy] + xs[dx]) * nz + z_ex[dz]
-                    remote(
-                        key_send.at[ee], key_recv.at[ex], send_sem.at[6], recv_sem.at[6],
-                        {"dp": dp, "expert": ee},
-                    ).start()
+    for dy, dx, dz in spread_offsets((ny, nx, nz))[1:]:
+        ee = (ys[dy] + xs[dx]) * nz + z_ex[dz]
+        remote(
+            key_send.at[ee], key_recv.at[ex], send_sem.at[6], recv_sem.at[6],
+            {"dp": dp, "expert": ee},
+        ).start()
     key_recv[ex] = key_send[ex]
     most = pl.ds(0, experts - 1)
 

time: 59.5 us -> 59.8 us (level)
  no operation moved by 1% of the time
where the time goes in v3:
time: 59.8 us; the launch traced here: 59.6 us
  Pallas kernels  58.3 us (97%)
  between operations  1.29 us (2%)
    pallas_call x1, Pallas kernels, slots(): pl.pallas_call(functools.partial(slot_kernel, sizes), out_shape=(vmem((im...  54 us
    pallas_call x1, Pallas kernels, stored(): pl.pallas_call(store_kernel, out_shape=tuple((shape(one.shape, one.dtype)...  4.36 us

profile of v3, /device:TPU:1, one launch (start us, length us, event | category | flops | bytes accessed | tf_op | source)
XLA Modules:
  0.0 59.6 jit_solution(13598786579180661968)
XLA Ops:
  1.3 54.0 %slots.1 = (bf16[2,512,1408]{2,1,0:T(8,128)(2,1)S(1)}, bf16[1,1408,1536]{2,1,0:T(8,128)(2,1)S(1)}, bf16[1,1536,1408]{2,1,0:T(8,128)(2,1)S(1)}, f32[1,1408]{1,0:T(1,128)S(1)}) custom-call(bf16[2,512,1408]{2,1,0:T(8,128)(2,1)} %tok_h.1, bf16[2,512,1408]{2,1,0:T(8,128)(2,1)} %cot_h.1, bf16[1,1408,1536]{2,1,0:T(8,128)(2,1)} %w1_h.1, ...), custom_call_target="tpu_custom_call" | custom-call | flops 4429185024 | bytes 11534336 | tf_op jit(solution)/shard_map/slots/pallas_call | solution.py:418
  55.3 4.4 %stored.1 = (bf16[2,512,1408]{2,1,0:T(8,128)(2,1)}, bf16[1,1408,1536]{2,1,0:T(8,128)(2,1)}, bf16[1,1536,1408]{2,1,0:T(8,128)(2,1)}, f32[1,1408]{1,0:T(1,128)}) custom-call(bf16[2,512,1408]{2,1,0:T(8,128)(2,1)S(1)} %get-tuple-element.12.gt, bf16[1,1408,1536]{2,1,0:T(8,128)(2,1)S(1)} %get-tuple-element.13.gi, bf16[1,1536,1408]{2,1,0:T(8,128)(2,1)S(1)} %get-tuple-element.14.go, ...), custom_call_target="tpu_custom_call" | custom-call | bytes 11537152 | tf_op jit(solution)/shard_map/stored/pallas_call | solution.py:507

commit v4 on v3

--- a/solution.py
+++ b/solution.py
@@ -104,12 +104,23 @@
     def load(index, src, dst):
         return pltpu.make_async_copy(src, dst, load_sem.at[index])
 
-    loads = [load(b, tok_h.at[b], tok.at[pl.ds(b * tokens, tokens)]) for b in range(images)]
-    loads += [
-        load(images + b, cot_h.at[b], cot.at[pl.ds(b * tokens, tokens)]) for b in range(images)
+    pieces = 2
+    piece = tokens // pieces
+    tok_loads = [
+        load(
+            b * pieces + p, tok_h.at[b, pl.ds(p * piece, piece)],
+            tok.at[pl.ds(b * tokens + p * piece, piece)],
+        )
+        for b in range(images)
+        for p in range(pieces)
     ]
-    loads += [load(2 * images, w1_h.at[0], w1), load(2 * images + 1, w2_h.at[0], w2)]
-    for one in loads[: 2 * images]:
+    done = images * pieces
+    cot_loads = [
+        load(done + b, cot_h.at[b], cot.at[pl.ds(b * tokens, tokens)]) for b in range(images)
+    ]
+    done += images
+    weight_loads = [load(done, w1_h.at[0], w1), load(done + 1, w2_h.at[0], w2)]
+    for one in tok_loads:
         one.start()
 
     barrier = pltpu.get_barrier_semaphore()
@@ -130,22 +141,27 @@
     ).astype(BF16)
 
     for b in range(images):
-        loads[b].wait()
-        if b == 0:
-            loads[2 * images].start()
-            loads[2 * images + 1].start()
         rows = pl.ds(b * tokens, tokens)
-        for i in range(tokens // 128):
-            part = tok[b * tokens + i * 128 : b * tokens + (i + 1) * 128, :].astype(F32)
-            square = part * part
-            acc = square[:, :128]
-            for j in range(1, width // 128):
-                acc = acc + square[:, j * 128 : (j + 1) * 128]
-            rinv_s[b, :, i * 128 : (i + 1) * 128] = lax.rsqrt(
-                jnp.sum(acc.T, axis=0, keepdims=True) + EPS
-            )
-            down = lax.rsqrt(jnp.sum(acc, axis=1, keepdims=True) + EPS)
-            normed[i * 128 : (i + 1) * 128, :] = (part * down).astype(BF16)
+        for p in range(pieces):
+            tok_loads[b * pieces + p].wait()
+            if b == 0 and p == 0:
+                for one in (*cot_loads, *weight_loads):
+                    one.start()
+            for i in range(p * piece // 128, (p + 1) * piece // 128):
+                accs = []
+                for r in range(i * 128, (i + 1) * 128, 32):
+                    part = tok[b * tokens + r : b * tokens + r + 32, :].astype(F32)
+                    square = part * part
+                    acc = square[:, :128]
+                    for j in range(1, width // 128):
+                        acc = acc + square[:, j * 128 : (j + 1) * 128]
+                    accs.append(acc)
+                    down = lax.rsqrt(jnp.sum(acc, axis=1, keepdims=True) + EPS)
+                    normed[r : r + 32, :] = (part * down).astype(BF16)
+                acc = jnp.concatenate(accs, axis=0)
+                rinv_s[b, :, i * 128 : (i + 1) * 128] = lax.rsqrt(
+                    jnp.sum(acc.T, axis=0, keepdims=True) + EPS
+                )
         logits = dot(keysn[...], normed[...], NT) * scale
         expo = jnp.exp(logits)
         disp = expo / jnp.sum(expo, axis=1, keepdims=True)
@@ -185,8 +201,8 @@
     unpack(send_in, dot(mix_in[...], tok[...]).astype(BF16))
     pl.semaphore_wait(barrier, near + 1)
     out_of_experts(0, send_in, recv_in)
-    for b in range(images):
-        loads[images + b].wait()
+    for one in cot_loads:
+        one.wait()
     unpack(send_grad, dot(mix_grad[...], cot[...]).astype(BF16))
     out_of_experts(1, send_grad, recv_grad)
 
@@ -208,8 +224,8 @@
         return copies
 
     copies_in = arrive(0, recv_in, x)
-    loads[2 * images].wait()
-    loads[2 * images + 1].wait()
+    for one in weight_loads:
+        one.wait()
     for one in copies_in:
         one.wait_recv()
 
@@ -244,8 +260,6 @@
     lax.fori_loop(0, parts, second, 0)
 
     copies_grad = arrive(1, recv_grad, gs)
-    for one in copies_grad:
-        one.wait_recv()
 
     def third(j, carry):
         cols = pl.ds(pl.multiple_of(j * step, step), step)
@@ -270,6 +284,8 @@
         in_ref[0] = out_ref[0]
 
     chip_sums(0, own_out, pair_out_r, rows_out, send_out, recv_out)
+    for one in copies_grad:
+        one.wait_recv()
     lax.fori_loop(0, hidden // step, third, 0, unroll=2)
 
     def fourth(j, carry):
@@ -362,9 +378,9 @@
     most = pl.ds(0, experts - 1)
 
     per = min(256, tokens)
-    for b in range(images):
-
-        def one(j, carry, b=b):
+
+    def token_grads(b):
+        def one(j, carry):
             cut = pl.ds(pl.multiple_of(j * per, per), per)
             rows = pl.ds(pl.multiple_of(b * tokens + j * per, per), per)
             res = dot(at[b, :, cut], mix_b[b], TN)
@@ -376,6 +392,8 @@
 
         lax.fori_loop(0, tokens // per, one, 0)
 
+    for b in range(images // 2):
+        token_grads(b)
     wait_for(key_recv.at[most], recv_sem.at[6])
     total = key_recv[0]
     for e in range(1, experts):
@@ -386,6 +404,8 @@
             key_tot.at[dp], key_tot.at[dp], send_sem.at[7], recv_sem.at[7],
             {"dp": (dp + k) % 4, "expert": ex},
         ).start()
+    for b in range(images // 2, images):
+        token_grads(b)
     wait_for(key_tot.at[pl.ds(0, 3)], recv_sem.at[7])
     grad = (key_tot[0] + key_tot[1]) + (key_tot[2] + key_tot[3])
     own = kt[pl.ds(ex, 1), :]
@@ -468,7 +488,7 @@
             vmem((experts, 1, width), F32),
             vmem((experts, 1, width), F32),
             vmem((4, 1, width), F32),
-            dma((2 * images + 2,)),
+            dma((3 * images + 2,)),
             dma((8,)),
             dma((8,)),
             dma((4, ny)),

time: 59.8 us -> 59.5 us (level)
  no operation moved by 1% of the time
where the time goes in v4:
time: 59.5 us; the launch traced here: 59.3 us
  Pallas kernels  58 us (97%)
  between operations  1.29 us (2%)
    pallas_call x1, Pallas kernels, slots(): pl.pallas_call(functools.partial(slot_kernel, sizes), out_shape=(vmem((im...  53.7 us
    pallas_call x1, Pallas kernels, stored(): pl.pallas_call(store_kernel, out_shape=tuple((shape(one.shape, one.dtype)...  4.36 us

profile of v4, /device:TPU:1, one launch (start us, length us, event | category | flops | bytes accessed | tf_op | source)
XLA Modules:
  0.0 59.3 jit_solution(8622844982676844034)
XLA Ops:
  1.3 53.7 %slots.1 = (bf16[2,512,1408]{2,1,0:T(8,128)(2,1)S(1)}, bf16[1,1408,1536]{2,1,0:T(8,128)(2,1)S(1)}, bf16[1,1536,1408]{2,1,0:T(8,128)(2,1)S(1)}, f32[1,1408]{1,0:T(1,128)S(1)}) custom-call(bf16[2,512,1408]{2,1,0:T(8,128)(2,1)} %tok_h.1, bf16[2,512,1408]{2,1,0:T(8,128)(2,1)} %cot_h.1, bf16[1,1408,1536]{2,1,0:T(8,128)(2,1)} %w1_h.1, ...), custom_call_target="tpu_custom_call" | custom-call | flops 4429185024 | bytes 11534336 | tf_op jit(solution)/shard_map/slots/pallas_call | solution.py:438
  55.0 4.4 %stored.1 = (bf16[2,512,1408]{2,1,0:T(8,128)(2,1)}, bf16[1,1408,1536]{2,1,0:T(8,128)(2,1)}, bf16[1,1536,1408]{2,1,0:T(8,128)(2,1)}, f32[1,1408]{1,0:T(1,128)}) custom-call(bf16[2,512,1408]{2,1,0:T(8,128)(2,1)S(1)} %get-tuple-element.12.gt, bf16[1,1408,1536]{2,1,0:T(8,128)(2,1)S(1)} %get-tuple-element.13.gi, bf16[1,1536,1408]{2,1,0:T(8,128)(2,1)S(1)} %get-tuple-element.14.go, ...), custom_call_target="tpu_custom_call" | custom-call | bytes 11537152 | tf_op jit(solution)/shard_map/stored/pallas_call | solution.py:527

commit v5 on v4

--- a/solution.py
+++ b/solution.py
@@ -318,9 +318,6 @@
 
     turn(act, actt, hidden)
     product(actt, gs, go_o, hidden // 4)
-    turn(x, xt, width)
-    product(xt, pg, gi_o, width // 4)
-
     def collect(kind, in_ref, rows_ref):
         for group in range(ny):
             count = layer if group else layer - 1
@@ -392,6 +389,8 @@
 
         lax.fori_loop(0, tokens // per, one, 0)
 
+    turn(x, xt, width)
+    product(xt, pg, gi_o, width // 4)
     for b in range(images // 2):
         token_grads(b)
     wait_for(key_recv.at[most], recv_sem.at[6])

time: 59.5 us -> 59.2 us (level)
  no operation moved by 1% of the time
where the time goes in v5:
time: 59.2 us; the launch traced here: 59 us
  Pallas kernels  57.7 us (97%)
  between operations  1.29 us (2%)
    pallas_call x1, Pallas kernels, slots(): pl.pallas_call(functools.partial(slot_kernel, sizes), out_shape=(vmem((im...  53.4 us
    pallas_call x1, Pallas kernels, stored(): pl.pallas_call(store_kernel, out_shape=tuple((shape(one.shape, one.dtype)...  4.36 us

profile of v5, /device:TPU:1, one launch (start us, length us, event | category | flops | bytes accessed | tf_op | source)
XLA Modules:
  0.0 59.0 jit_solution(13437095779665731984)
XLA Ops:
  1.3 53.4 %slots.1 = (bf16[2,512,1408]{2,1,0:T(8,128)(2,1)S(1)}, bf16[1,1408,1536]{2,1,0:T(8,128)(2,1)S(1)}, bf16[1,1536,1408]{2,1,0:T(8,128)(2,1)S(1)}, f32[1,1408]{1,0:T(1,128)S(1)}) custom-call(bf16[2,512,1408]{2,1,0:T(8,128)(2,1)} %tok_h.1, bf16[2,512,1408]{2,1,0:T(8,128)(2,1)} %cot_h.1, bf16[1,1408,1536]{2,1,0:T(8,128)(2,1)} %w1_h.1, ...), custom_call_target="tpu_custom_call" | custom-call | flops 4429185024 | bytes 11534336 | tf_op jit(solution)/shard_map/slots/pallas_call | solution.py:437
  54.6 4.4 %stored.1 = (bf16[2,512,1408]{2,1,0:T(8,128)(2,1)}, bf16[1,1408,1536]{2,1,0:T(8,128)(2,1)}, bf16[1,1536,1408]{2,1,0:T(8,128)(2,1)}, f32[1,1408]{1,0:T(1,128)}) custom-call(bf16[2,512,1408]{2,1,0:T(8,128)(2,1)S(1)} %get-tuple-element.12.gt, bf16[1,1408,1536]{2,1,0:T(8,128)(2,1)S(1)} %get-tuple-element.13.gi, bf16[1,1536,1408]{2,1,0:T(8,128)(2,1)S(1)} %get-tuple-element.14.go, ...), custom_call_target="tpu_custom_call" | custom-call | bytes 11537152 | tf_op jit(solution)/shard_map/stored/pallas_call | solution.py:526

commit v6 on v5

--- a/solution.py
+++ b/solution.py
@@ -55,7 +55,8 @@
         order.append(best)
         for kind in enumerate(best):
             used[kind] += 1
-    return order
+    near = lambda one: sum(min(d, n - d) for d, n in zip(one, dims))
+    return order[:1] + sorted(order[1:], key=near, reverse=True)
 
 
 def slot_kernel(
@@ -120,9 +121,6 @@
     ]
     done += images
     weight_loads = [load(done, w1_h.at[0], w1), load(done + 1, w2_h.at[0], w2)]
-    for one in tok_loads:
-        one.start()
-
     barrier = pltpu.get_barrier_semaphore()
 
     def greet(p, ee, device):
@@ -133,6 +131,9 @@
         pl.semaphore_signal(
             barrier, inc=1, device_id={"dp": far * 2 + 1 - core, "expert": ex}, device_id_type=MESH
         )
+
+    for one in tok_loads:
+        one.start()
 
     key_rows = keys_ref[...].astype(F32)
     kt[...] = key_rows

time: 59.2 us -> 56.4 us (0.953)
  Pallas kernels: 57.7 us -> 55 us
    pallas_call x1, Pallas kernels: 53.4 us -> 50.6 us  [slots(): pl.pallas_call(functools.partial(slot_kernel, sizes), out_shape=(vmem((im...]
where the time goes in v6:
time: 56.4 us; the launch traced here: 56.3 us
  Pallas kernels  55 us (98%)
  between operations  1.29 us (2%)
    pallas_call x1, Pallas kernels, slots(): pl.pallas_call(functools.partial(slot_kernel, sizes), out_shape=(vmem((im...  50.6 us
    pallas_call x1, Pallas kernels, stored(): pl.pallas_call(store_kernel, out_shape=tuple((shape(one.shape, one.dtype)...  4.36 us

profile of v6, /device:TPU:1, one launch (start us, length us, event | category | flops | bytes accessed | tf_op | source)
XLA Modules:
  0.0 56.3 jit_solution(17445723576699707557)
XLA Ops:
  1.3 50.6 %slots.1 = (bf16[2,512,1408]{2,1,0:T(8,128)(2,1)S(1)}, bf16[1,1408,1536]{2,1,0:T(8,128)(2,1)S(1)}, bf16[1,1536,1408]{2,1,0:T(8,128)(2,1)S(1)}, f32[1,1408]{1,0:T(1,128)S(1)}) custom-call(bf16[2,512,1408]{2,1,0:T(8,128)(2,1)} %tok_h.1, bf16[2,512,1408]{2,1,0:T(8,128)(2,1)} %cot_h.1, bf16[1,1408,1536]{2,1,0:T(8,128)(2,1)} %w1_h.1, ...), custom_call_target="tpu_custom_call" | custom-call | flops 4429185024 | bytes 11534336 | tf_op jit(solution)/shard_map/slots/pallas_call | solution.py:438
  51.9 4.4 %stored.1 = (bf16[2,512,1408]{2,1,0:T(8,128)(2,1)}, bf16[1,1408,1536]{2,1,0:T(8,128)(2,1)}, bf16[1,1536,1408]{2,1,0:T(8,128)(2,1)}, f32[1,1408]{1,0:T(1,128)}) custom-call(bf16[2,512,1408]{2,1,0:T(8,128)(2,1)S(1)} %get-tuple-element.12.gt, bf16[1,1408,1536]{2,1,0:T(8,128)(2,1)S(1)} %get-tuple-element.13.gi, bf16[1,1536,1408]{2,1,0:T(8,128)(2,1)S(1)} %get-tuple-element.14.go, ...), custom_call_target="tpu_custom_call" | custom-call | bytes 11537152 | tf_op jit(solution)/shard_map/stored/pallas_call | solution.py:527

commit v7 on v6

--- a/solution.py
+++ b/solution.py
@@ -272,17 +272,17 @@
         for j in range(parts):
             start = min(j * wide, width - wide)
             rows_ref[:, start : start + wide] = (own[j] + pair_r[j].astype(F32)).astype(BF16)
-        for p in range(near):
-            out_ref[p] = rows_ref[p * images : (p + 1) * images, :]
-
         def one(p, ee, device):
+            if p % layer == 1:
+                for i in range(p, min(p + layer, near)):
+                    out_ref[i] = rows_ref[i * images : (i + 1) * images, :]
             remote(
                 out_ref.at[p], in_ref.at[p], send_sem.at[2 + kind], in_sem.at[2 + kind, p // layer],
                 device,
             ).start()
 
         each_partner(one, -1)
-        in_ref[0] = out_ref[0]
+        in_ref[0] = rows_ref[:images, :]
 
     chip_sums(0, own_out, pair_out_r, rows_out, send_out, recv_out)
     for one in copies_grad:

time: 56.4 us -> 56.3 us (level)
  no operation moved by 1% of the time
where the time goes in v7:
time: 56.3 us; the launch traced here: 56.2 us
  Pallas kernels  54.9 us (98%)
  between operations  1.29 us (2%)
    pallas_call x1, Pallas kernels, slots(): pl.pallas_call(functools.partial(slot_kernel, sizes), out_shape=(vmem((im...  50.5 us
    pallas_call x1, Pallas kernels, stored(): pl.pallas_call(store_kernel, out_shape=tuple((shape(one.shape, one.dtype)...  4.36 us

profile of v7, /device:TPU:1, one launch (start us, length us, event | category | flops | bytes accessed | tf_op | source)
XLA Modules:
  0.0 56.2 jit_solution(9441515564735323458)
XLA Ops:
  1.3 50.5 %slots.1 = (bf16[2,512,1408]{2,1,0:T(8,128)(2,1)S(1)}, bf16[1,1408,1536]{2,1,0:T(8,128)(2,1)S(1)}, bf16[1,1536,1408]{2,1,0:T(8,128)(2,1)S(1)}, f32[1,1408]{1,0:T(1,128)S(1)}) custom-call(bf16[2,512,1408]{2,1,0:T(8,128)(2,1)} %tok_h.1, bf16[2,512,1408]{2,1,0:T(8,128)(2,1)} %cot_h.1, bf16[1,1408,1536]{2,1,0:T(8,128)(2,1)} %w1_h.1, ...), custom_call_target="tpu_custom_call" | custom-call | flops 4429185024 | bytes 11534336 | tf_op jit(solution)/shard_map/slots/pallas_call | solution.py:438
  51.8 4.4 %stored.1 = (bf16[2,512,1408]{2,1,0:T(8,128)(2,1)}, bf16[1,1408,1536]{2,1,0:T(8,128)(2,1)}, bf16[1,1536,1408]{2,1,0:T(8,128)(2,1)}, f32[1,1408]{1,0:T(1,128)}) custom-call(bf16[2,512,1408]{2,1,0:T(8,128)(2,1)S(1)} %get-tuple-element.12.gt, bf16[1,1408,1536]{2,1,0:T(8,128)(2,1)S(1)} %get-tuple-element.13.gi, bf16[1,1536,1408]{2,1,0:T(8,128)(2,1)S(1)} %get-tuple-element.14.go, ...), custom_call_target="tpu_custom_call" | custom-call | bytes 11537152 | tf_op jit(solution)/shard_map/stored/pallas_call | solution.py:527

commit v8 on v7

--- a/solution.py
+++ b/solution.py
@@ -205,7 +205,6 @@
     for one in cot_loads:
         one.wait()
     unpack(send_grad, dot(mix_grad[...], cot[...]).astype(BF16))
-    out_of_experts(1, send_grad, recv_grad)
 
     def arrive(kind, in_ref, rows_ref):
         copies = []
@@ -225,6 +224,7 @@
         return copies
 
     copies_in = arrive(0, recv_in, x)
+    out_of_experts(1, send_grad, recv_grad)
     for one in weight_loads:
         one.wait()
     for one in copies_in:
@@ -259,8 +259,6 @@
         return carry
 
     lax.fori_loop(0, parts, second, 0)
-
-    copies_grad = arrive(1, recv_grad, gs)
 
     def third(j, carry):
         cols = pl.ds(pl.multiple_of(j * step, step), step)
@@ -285,6 +283,7 @@
         in_ref[0] = rows_ref[:images, :]
 
     chip_sums(0, own_out, pair_out_r, rows_out, send_out, recv_out)
+    copies_grad = arrive(1, recv_grad, gs)
     for one in copies_grad:
         one.wait_recv()
     lax.fori_loop(0, hidden // step, third, 0, unroll=2)

time: 56.3 us -> 57.3 us (1.018)
  Pallas kernels: 54.9 us -> 55.8 us
    pallas_call x1, Pallas kernels: 50.5 us -> 51.5 us  [slots(): pl.pallas_call(functools.partial(slot_kernel, sizes), out_shape=(vmem((im...]
where the time goes in v8:
time: 57.3 us; the launch traced here: 57.1 us
  Pallas kernels  55.8 us (97%)
  between operations  1.29 us (2%)
    pallas_call x1, Pallas kernels, slots(): pl.pallas_call(functools.partial(slot_kernel, sizes), out_shape=(vmem((im...  51.5 us
    pallas_call x1, Pallas kernels, stored(): pl.pallas_call(store_kernel, out_shape=tuple((shape(one.shape, one.dtype)...  4.36 us

profile of v8, /device:TPU:1, one launch (start us, length us, event | category | flops | bytes accessed | tf_op | source)
XLA Modules:
  0.0 57.1 jit_solution(6287141807774157668)
XLA Ops:
  1.3 51.5 %slots.1 = (bf16[2,512,1408]{2,1,0:T(8,128)(2,1)S(1)}, bf16[1,1408,1536]{2,1,0:T(8,128)(2,1)S(1)}, bf16[1,1536,1408]{2,1,0:T(8,128)(2,1)S(1)}, f32[1,1408]{1,0:T(1,128)S(1)}) custom-call(bf16[2,512,1408]{2,1,0:T(8,128)(2,1)} %tok_h.1, bf16[2,512,1408]{2,1,0:T(8,128)(2,1)} %cot_h.1, bf16[1,1408,1536]{2,1,0:T(8,128)(2,1)} %w1_h.1, ...), custom_call_target="tpu_custom_call" | custom-call | flops 4429185024 | bytes 11534336 | tf_op jit(solution)/shard_map/slots/pallas_call | solution.py:437
  52.8 4.4 %stored.1 = (bf16[2,512,1408]{2,1,0:T(8,128)(2,1)}, bf16[1,1408,1536]{2,1,0:T(8,128)(2,1)}, bf16[1,1536,1408]{2,1,0:T(8,128)(2,1)}, f32[1,1408]{1,0:T(1,128)}) custom-call(bf16[2,512,1408]{2,1,0:T(8,128)(2,1)S(1)} %get-tuple-element.12.gt, bf16[1,1408,1536]{2,1,0:T(8,128)(2,1)S(1)} %get-tuple-element.13.gi, bf16[1,1536,1408]{2,1,0:T(8,128)(2,1)S(1)} %get-tuple-element.14.go, ...), custom_call_target="tpu_custom_call" | custom-call | bytes 11537152 | tf_op jit(solution)/shard_map/stored/pallas_call | solution.py:526

commit v9 on v7

--- a/solution.py
+++ b/solution.py
@@ -209,7 +209,7 @@
 
     def arrive(kind, in_ref, rows_ref):
         copies = []
-        for group in range(ny):
+        for group in reversed(range(ny)):
             count = layer if group else layer - 1
             wait_for(in_ref.at[pl.ds(0, count)], in_sem.at[kind, group])
             pack(rows_ref, group * layer * images, in_ref, group * layer, layer)
@@ -320,7 +320,7 @@
     turn(act, actt, hidden)
     product(actt, gs, go_o, hidden // 4)
     def collect(kind, in_ref, rows_ref):
-        for group in range(ny):
+        for group in reversed(range(ny)):
             count = layer if group else layer - 1
             wait_for(in_ref.at[pl.ds(0, count)], in_sem.at[2 + kind, group])
             pack(rows_ref, group * layer * images, in_ref, group * layer, layer)

time: 56.3 us -> 56.8 us (level)
  no operation moved by 1% of the time
where the time goes in v9:
time: 56.8 us; the launch traced here: 56.7 us
  Pallas kernels  55.4 us (98%)
  between operations  1.29 us (2%)
    pallas_call x1, Pallas kernels, slots(): pl.pallas_call(functools.partial(slot_kernel, sizes), out_shape=(vmem((im...  51 us
    pallas_call x1, Pallas kernels, stored(): pl.pallas_call(store_kernel, out_shape=tuple((shape(one.shape, one.dtype)...  4.36 us

profile of v9, /device:TPU:1, one launch (start us, length us, event | category | flops | bytes accessed | tf_op | source)
XLA Modules:
  0.0 56.7 jit_solution(15750860273643732023)
XLA Ops:
  1.3 51.0 %slots.1 = (bf16[2,512,1408]{2,1,0:T(8,128)(2,1)S(1)}, bf16[1,1408,1536]{2,1,0:T(8,128)(2,1)S(1)}, bf16[1,1536,1408]{2,1,0:T(8,128)(2,1)S(1)}, f32[1,1408]{1,0:T(1,128)S(1)}) custom-call(bf16[2,512,1408]{2,1,0:T(8,128)(2,1)} %tok_h.1, bf16[2,512,1408]{2,1,0:T(8,128)(2,1)} %cot_h.1, bf16[1,1408,1536]{2,1,0:T(8,128)(2,1)} %w1_h.1, ...), custom_call_target="tpu_custom_call" | custom-call | flops 4429185024 | bytes 11534336 | tf_op jit(solution)/shard_map/slots/pallas_call | solution.py:438
  52.3 4.4 %stored.1 = (bf16[2,512,1408]{2,1,0:T(8,128)(2,1)}, bf16[1,1408,1536]{2,1,0:T(8,128)(2,1)}, bf16[1,1536,1408]{2,1,0:T(8,128)(2,1)}, f32[1,1408]{1,0:T(1,128)}) custom-call(bf16[2,512,1408]{2,1,0:T(8,128)(2,1)S(1)} %get-tuple-element.12.gt, bf16[1,1408,1536]{2,1,0:T(8,128)(2,1)S(1)} %get-tuple-element.13.gi, bf16[1,1536,1408]{2,1,0:T(8,128)(2,1)S(1)} %get-tuple-element.14.go, ...), custom_call_target="tpu_custom_call" | custom-call | bytes 11537152 | tf_op jit(solution)/shard_map/stored/pallas_call | solution.py:527
